TPU v7x, 256 devices: a whole 4x4x8 slice. The times are simulated.
256 devices in a mesh: dp: 4 (over x), expert: 64 (over y, z, core).
Axes of the slice: x: 4, y: 4, z: 8, core: 2. Of those that a mesh axis runs over, the one named last changes fastest.
Arguments:
- tokens: bfloat16 [32768, 2048], P(('dp', 'expert')), may hold values from -6 to 6
- expert_ids: int32 [32768, 4], P(('dp', 'expert')), may hold values from 0 to 63, all different within a row; in each aligned block of 128 rows (0 to 127, 128 to 255, ...) at most 10 rows name the same one
- probs: float32 [32768, 4], P(('dp', 'expert')), may hold values from 0.2 to 1
- trade: int32 [32], replicated, may hold values from 0 to 1, as said below
- gate_weight: bfloat16 [64, 2048, 768], P('expert'), may hold values from -0.125 to 0.125
- up_weight: bfloat16 [64, 2048, 768], P('expert'), may hold values from -0.125 to 0.125
- down_weight: bfloat16 [64, 768, 2048], P('expert'), may hold values from -0.21875 to 0.21875
- out_grad: bfloat16 [32768, 2048], P(('dp', 'expert')), may hold values from -0.29882812 to 0.29882812
Outputs:
- combined: bfloat16 [32768, 2048], P(('dp', 'expert'))
- gate_grad: bfloat16 [64, 2048, 768], P('expert', 'dp')
- up_grad: bfloat16 [64, 2048, 768], P('expert', 'dp')
- down_grad: bfloat16 [64, 768, 2048], P('expert', None, 'dp')
Inputs may be any that keep to these rules, and one draw needn't show every extreme that they name: `trade`: index k below 32 pairs expert index k with k + 32; at least one pair trades and at least one does not. `expert_ids`: each row names 4 different experts. Within the 128 rows of one device no expert is named by more than 10 rows, a bound that some block reaches.
All inputs are finite; a program needn't handle non-finite values.
Results may differ from a plain program's by a relative error of at most 0.0095.
Values may be sent and summed in bfloat16 or wider, within the bound.
No kernel may reach another device: no remote copies, remote signals or barrier semaphores. Data moves between devices by JAX's collectives and lax.ppermute only.
A program may use at most 128 MiB of HBM per device.

v0:
```python
import jax
import jax.numpy as jnp
from jax import lax
from jax.sharding import Mesh
from jax.sharding import PartitionSpec as P

Y, Z, C = "expert_y", "expert_z", "expert_c"
EXPERT = (Y, Z, C)
DP_EXPERT = ("dp",) + EXPERT
F32, BF16, I32 = jnp.float32, jnp.bfloat16, jnp.int32


def dot(a, b, dims=((1,), (0,))):
    return lax.dot_general(a, b, (dims, ((), ())), preferred_element_type=F32)


def local(tokens, expert_ids, probs, trade, gate_weight, up_weight, down_weight, out_grad):
    tok_count, width = tokens.shape
    top_count = expert_ids.shape[1]
    ny, nz, nc = (lax.axis_size(a) for a in EXPERT)
    experts = ny * nz * nc
    halfway = experts // 2
    cap = 5 * tok_count * top_count // (4 * experts)
    peers = ny * nc
    block = nz * cap
    rows = peers * block
    ndp = lax.axis_size("dp")

    all_tokens = lax.all_gather(tokens, Z, axis=0, tiled=True)
    all_grads = lax.all_gather(out_grad, Z, axis=0, tiled=True)

    numbers = jnp.arange(experts, dtype=I32)
    traded = jnp.concatenate([trade, trade]) == 1
    owners = jnp.where(traded, jnp.bitwise_xor(numbers, halfway), numbers)
    ids_t = expert_ids.T
    probs_t = probs.T
    hits = ids_t[:, None, :] == owners[None, :, None]
    named = jnp.any(hits, axis=0)
    weight = jnp.sum(jnp.where(hits, probs_t[:, None, :], 0.0), axis=0)
    before = (
        lax.broadcasted_iota(I32, (tok_count, tok_count), 0)
        < lax.broadcasted_iota(I32, (tok_count, tok_count), 1)
    ).astype(BF16)
    rank = jnp.where(named, dot(named.astype(BF16), before), -1.0)
    by_z = lambda a: a.reshape(ny, nz, nc, tok_count).transpose(1, 0, 2, 3).reshape(nz, peers, tok_count)
    rank_z, weight_z = by_z(rank), by_z(weight)
    info = lax.all_to_all(jnp.concatenate([rank_z, weight_z], axis=1), Z, 0, 0, tiled=True)
    src_rank, src_weight = info[:, :peers], info[:, peers:]
    row_of = jnp.where(
        src_rank >= 0, src_rank + (jnp.arange(nz, dtype=F32) * cap)[:, None, None], -1.0
    ).astype(I32)
    row_of = row_of.transpose(1, 0, 2).reshape(peers, nz * tok_count)
    weight_of = src_weight.transpose(1, 0, 2).reshape(peers, nz * tok_count)
    match = row_of[:, None, :] == jnp.arange(block, dtype=I32)[None, :, None]
    pick = match.astype(BF16).reshape(rows, nz * tok_count)
    row_weight = jnp.sum(jnp.where(match, weight_of[:, None, :], 0.0), axis=2).reshape(rows, 1)

    swap = lambda a: lax.all_to_all(
        a.reshape(peers, block, width), (Y, C), 0, 0, tiled=True
    ).reshape(rows, width)

    expert_rows = swap(dot(pick, all_tokens).astype(BF16))
    out_rows = swap((row_weight * dot(pick, all_grads)).astype(BF16))

    w_gate, w_up, w_down = gate_weight[0], up_weight[0], down_weight[0]
    gate_act = dot(expert_rows, w_gate)
    up_act = dot(expert_rows, w_up)
    sigma = jax.nn.sigmoid(gate_act)
    silu = gate_act * sigma
    hidden = (silu * up_act).astype(BF16)
    expert_out = dot(hidden, w_down).astype(BF16)

    returned = swap(expert_out)
    to = lax.broadcasted_iota(I32, (rows, rows), 0)
    at = lax.broadcasted_iota(I32, (rows, rows), 1)
    moved = (at // block) * cap + (at % block) // cap * (peers * cap) + at % cap
    regroup = (to == moved).astype(BF16)
    returned = dot(regroup, returned).astype(BF16).reshape(nz, peers * cap, width)
    home = lax.all_to_all(returned, Z, 0, 0, tiled=True).reshape(rows, width)
    spread = jnp.where(
        rank_z[:, :, None, :] == jnp.arange(cap, dtype=F32)[None, None, :, None],
        weight_z[:, :, None, :],
        0.0,
    ).reshape(rows, tok_count)
    high = spread.astype(BF16)
    low = (spread - high.astype(F32)).astype(BF16)
    dims = ((0,), (0,))
    combined = (dot(high, home, dims) + dot(low, home, dims)).astype(BF16)

    hidden_grad = dot(out_rows, w_down, ((1,), (1,)))
    gate_back = (hidden_grad * up_act * (sigma * (1.0 + gate_act * (1.0 - sigma)))).astype(BF16)
    up_back = (hidden_grad * silu).astype(BF16)

    share = lambda a: lax.psum_scatter(a, "dp", scatter_dimension=0, tiled=True)
    part = width // ndp
    down_pieces = jnp.stack(
        [dot(hidden, out_rows[:, d * part : (d + 1) * part], dims).astype(BF16) for d in range(ndp)]
    )
    down_part = share(down_pieces)
    gate_part = share(dot(expert_rows, gate_back, dims).astype(BF16))
    up_part = share(dot(expert_rows, up_back, dims).astype(BF16))
    return combined, gate_part[None], up_part[None], down_part


def solution(mesh):
    finer = Mesh(mesh.devices.reshape(mesh.shape["dp"], 4, 8, 2), DP_EXPERT)
    rows = P(DP_EXPERT, None)
    stored = P(EXPERT, None, None)
    return jax.shard_map(
        local,
        mesh=finer,
        in_specs=(rows, rows, rows, P(), stored, stored, stored, rows),
        out_specs=(rows, P(EXPERT, "dp", None), P(EXPERT, "dp", None), P(EXPERT, None, "dp")),
        check_vma=False,
    )
```

profile of v0, /device:TPU:6, one launch (start us, length us, event | category | flops | bytes accessed | tf_op | source)
XLA Modules:
  0.0 313.3 jit_solution(13170197549271255373)
XLA Ops:
  8.7 0.8 compare_select_fusion.1
  9.5 0.8 fusion.43
  11.8 8.5 %all-to-all-start = ((f32[8,16,128]{2,1,0:T(8,128)}), f32[8,16,128]{2,1,0:T(8,128)S(1)}, u32[]{:S(2)}, u32[]{:S(2)}) async-start(f32[8,16,128]{2,1,0:T(8,128)} %copy.25), calls=%async_computation | async-start | bytes 131072 | tf_op jit(solution)/shard_map/all_to_all | solution.py:47
  20.4 8.4 %all-to-all-done = f32[8,16,128]{2,1,0:T(8,128)S(1)} async-done(((f32[8,16,128]{2,1,0:T(8,128)}), f32[8,16,128]{2,1,0:T(8,128)S(1)}, u32[]{:S(2)}, u32[]{:S(2)}) %all-to-all-start) | async-done | bytes 65568 | tf_op jit(solution)/shard_map/all_to_all | solution.py:47
  28.9 1.3 bitcast_compare_fusion
  30.1 37.5 %all-gather.3.cloned.1.call-done = bf16[1024,2048]{1,0:T(8,128)(2,1)} async-done(((bf16[128,2048]{1,0:T(8,128)(2,1)}), bf16[1024,2048]{1,0:T(8,128)(2,1)}) %all-gather.3.cloned.1.call-update) | async-done | bytes 4194320 | tf_op jit(solution)/shard_map/all_gather | solution.py:29
  67.6 6.7 %convolution_convert_fusion.4 = bf16[640,2048]{1,0:T(8,128)(2,1)} fusion(pred[640,1024]{1,0:T(32,128)(4,1)} %bitcast_compare_fusion, bf16[1024,2048]{1,0:T(8,128)(2,1)} %all-gather.3.cloned.1.call-done), kind=kOutput, calls=%fused_computation.5 | convolution fusion | flops 2685665280 | bytes 7471104 | tf_op jit(solution)/shard_map/dot_general | solution.py:14
  74.4 4.4 %all-to-all-start.1 = ((bf16[8,80,2048]{2,1,0:T(8,128)(2,1)}), bf16[8,80,2048]{2,1,0:T(8,128)(2,1)}, u32[]{:S(2)}, u32[]{:S(2)}) async-start(bf16[8,80,2048]{2,1,0:T(8,128)(2,1)} %bitcast.73), calls=%async_computation.1 | async-start | bytes 5242880 | tf_op jit(solution)/shard_map/all_to_all | solution.py:58
  79.3 43.5 %all-gather.5.cloned.1.call-done = bf16[1024,2048]{1,0:T(8,128)(2,1)} async-done(((bf16[128,2048]{1,0:T(8,128)(2,1)}), bf16[1024,2048]{1,0:T(8,128)(2,1)}) %all-gather.5.cloned.1.call-update) | async-done | bytes 4194320 | tf_op jit(solution)/shard_map/all_gather | solution.py:30
  122.8 6.8 %multiply_convert_fusion = bf16[640,2048]{1,0:T(8,128)(2,1)} fusion(pred[640,1024]{1,0:T(32,128)(4,1)} %bitcast_compare_fusion, bf16[1024,2048]{1,0:T(8,128)(2,1)} %all-gather.5.cloned.1.call-done, f32[640]{0:T(1024)S(1)} %mul.54), kind=kOutput, calls=%fused_computation | convolution fusion | flops 2686976000 | bytes 7473664 | tf_op jit(solution)/shard_map/dot_general | solution.py:14
  129.7 4.4 %all-to-all-start.4 = ((bf16[8,80,2048]{2,1,0:T(8,128)(2,1)}), bf16[8,80,2048]{2,1,0:T(8,128)(2,1)}, u32[]{:S(2)}, u32[]{:S(2)}) async-start(bf16[8,80,2048]{2,1,0:T(8,128)(2,1)} %bitcast.74), calls=%async_computation.4 | async-start | bytes 5242880 | tf_op jit(solution)/shard_map/all_to_all | solution.py:58
  134.3 5.0 %fusion.5 = f32[640,768]{1,0:T(8,128)S(1)} fusion(bf16[640,2048]{1,0:T(8,128)(2,1)} %bitcast.13, bf16[1,2048,768]{2,1,0:T(8,128)(2,1)} %param.12), kind=kOutput, calls=%fused_computation.12 | convolution fusion | flops 2013265920 | bytes 7733248 | tf_op jit(solution)/shard_map/dot_general | solution.py:14
  139.3 1.3 copy-done.4
  140.6 5.6 %multiply_convert_fusion.3 = (bf16[640,768]{1,0:T(8,128)(2,1)}, f32[640,768]{1,0:T(8,128)}) fusion(f32[640,768]{1,0:T(8,128)S(1)} %fusion.5, bf16[640,2048]{1,0:T(8,128)(2,1)} %bitcast.13, bf16[1,2048,768]{2,1,0:T(8,128)(2,1)S(1)} %copy-done.2), kind=kOutput, calls=%fused_computation.25 | convolution fusion | flops 2016215040 | bytes 10682368 | tf_op jit(solution)/shard_map/dot_general | solution.py:14
  146.3 20.6 %all-to-all-done.4 = bf16[8,80,2048]{2,1,0:T(8,128)(2,1)} async-done(((bf16[8,80,2048]{2,1,0:T(8,128)(2,1)}), bf16[8,80,2048]{2,1,0:T(8,128)(2,1)}, u32[]{:S(2)}, u32[]{:S(2)}) %all-to-all-start.4) | async-done | bytes 2621472 | tf_op jit(solution)/shard_map/all_to_all | solution.py:58
  166.9 4.1 %fusion = f32[640,768]{1,0:T(8,128)S(1)} fusion(bf16[640,2048]{1,0:T(8,128)(2,1)} %bitcast.24, bf16[1,768,2048]{2,1,0:T(8,128)(2,1)S(1)} %copy-done), kind=kOutput, calls=%fused_computation.7 | convolution fusion | flops 2013265920 | bytes 7733248 | tf_op jit(solution)/shard_map/dot_general | solution.py:14
  171.0 1.4 copy-done.6
  172.4 6.3 %convolution_convert_fusion.1 = bf16[2048,768]{1,0:T(8,128)(2,1)} fusion(bf16[640,2048]{1,0:T(8,128)(2,1)} %bitcast.13, f32[640,768]{1,0:T(8,128)S(1)} %copy-done.5, f32[640,768]{1,0:T(8,128)S(1)} %fusion, f32[640,768]{1,0:T(8,128)S(1)} %copy-done.7), kind=kOutput, calls=%fused_computation.2 | convolution fusion | flops 2019753984 | bytes 11665408 | tf_op jit(solution)/shard_map/dot_general | solution.py:14
  179.0 7.4 %convolution_convert_fusion = bf16[2048,768]{1,0:T(8,128)(2,1)} fusion(bf16[640,2048]{1,0:T(8,128)(2,1)} %bitcast.13, f32[640,768]{1,0:T(8,128)} %copy-done.6, f32[640,768]{1,0:T(8,128)} %copy-done.4), kind=kOutput, calls=%fused_computation.1 | convolution fusion | flops 2017787904 | bytes 9699328 | tf_op jit(solution)/shard_map/dot_general | solution.py:14
  186.5 5.2 %convolution_convert_fusion.2 = bf16[640,2048]{1,0:T(8,128)(2,1)} fusion(bf16[640,768]{1,0:T(8,128)(2,1)} %get-tuple-element.6, bf16[1,768,2048]{2,1,0:T(8,128)(2,1)S(1)} %copy-done), kind=kOutput, calls=%fused_computation.3 | convolution fusion | flops 2014576640 | bytes 6750208 | tf_op jit(solution)/shard_map/dot_general | solution.py:14
  191.7 4.4 %all-to-all-start.2 = ((bf16[8,80,2048]{2,1,0:T(8,128)(2,1)}), bf16[8,80,2048]{2,1,0:T(8,128)(2,1)}, u32[]{:S(2)}, u32[]{:S(2)}) async-start(bf16[8,80,2048]{2,1,0:T(8,128)(2,1)} %bitcast.71), calls=%async_computation.2 | async-start | bytes 5242880 | tf_op jit(solution)/shard_map/all_to_all | solution.py:58
  196.2 2.3 fusion.21
  198.4 1.9 fusion.20
  200.3 1.9 fusion.19
  202.3 1.9 fusion.18
  204.2 1.9 pad_maximum_fusion
  206.1 22.8 %all-to-all-done.2 = bf16[8,80,2048]{2,1,0:T(8,128)(2,1)} async-done(((bf16[8,80,2048]{2,1,0:T(8,128)(2,1)}), bf16[8,80,2048]{2,1,0:T(8,128)(2,1)}, u32[]{:S(2)}, u32[]{:S(2)}) %all-to-all-start.2) | async-done | bytes 2621472 | tf_op jit(solution)/shard_map/all_to_all | solution.py:58
  228.9 5.2 %convolution_convert_fusion.3 = bf16[640,2048]{1,0:T(8,128)(2,1)} fusion(bf16[640,2048]{1,0:T(8,128)(2,1)} %bitcast.18, s32[640]{0:T(1024)S(1)} %get-tuple-element.8, s32[640]{0:T(1024)S(1)} %get-tuple-element.12, s32[640]{0:T(1024)S(1)} %get-tuple-element.10, s32[640]{0:T(1024)S(1)} %get-tuple-element.11, s32[640]{0:T(1024)S(1)} %get-tuple-element.9, ...), kind=kOutput, calls=%fused_computation.4 | convolution fusion | flops 1685585920 | bytes 5260160 | tf_op jit(solution)/shard_map/dot_general | solution.py:14
  234.2 4.4 %all-to-all-start.3 = ((bf16[8,80,2048]{2,1,0:T(8,128)(2,1)}), bf16[8,80,2048]{2,1,0:T(8,128)(2,1)}, u32[]{:S(2)}, u32[]{:S(2)}) async-start(bf16[8,80,2048]{2,1,0:T(8,128)(2,1)} %bitcast.72), calls=%async_computation.3 | async-start | bytes 5242880 | tf_op jit(solution)/shard_map/all_to_all | solution.py:79
  240.3 60.8 %all-to-all-done.3 = bf16[8,80,2048]{2,1,0:T(8,128)(2,1)} async-done(((bf16[8,80,2048]{2,1,0:T(8,128)(2,1)}), bf16[8,80,2048]{2,1,0:T(8,128)(2,1)}, u32[]{:S(2)}, u32[]{:S(2)}) %all-to-all-start.3) | async-done | bytes 2621472 | tf_op jit(solution)/shard_map/all_to_all | solution.py:79
  301.1 2.5 fusion.61
  303.6 3.1 %fusion.7 = bf16[128,2048]{1,0:T(8,128)(2,1)} fusion(f32[128,2048]{1,0:T(8,128)S(1)} %fusion.61, bf16[640,128]{1,0:T(8,128)(2,1)S(1)} %copy-done.1, bf16[640,2048]{1,0:T(8,128)(2,1)} %bitcast.20), kind=kOutput, calls=%fused_computation.22 | convolution fusion | flops 336068608 | bytes 4358144 | tf_op jit(solution)/shard_map/dot_general | solution.py:14
  (51 shorter events, 6.0 us)
Async XLA Ops:
  7.2 159.7 %copy-start = (bf16[1,768,2048]{2,1,0:T(8,128)(2,1)S(1)}, bf16[1,768,2048]{2,1,0:T(8,128)(2,1)}, u32[]{:S(2)}) copy-start(bf16[1,768,2048]{2,1,0:T(8,128)(2,1)} %param.14) | copy-start | bytes 9437188
  7.2 60.5 %all-gather.3.cloned.1.call-start = ((), (), s32[]{:S(2)}) async-start(), calls=%async_computation.8 | async-start | bytes 4718592 | tf_op jit(solution)/shard_map/all_gather | solution.py:29
  7.9 114.9 %all-gather.5.cloned.1.call-start = ((), (), s32[]{:S(2)}) async-start(), calls=%async_computation.9 | async-start | bytes 4718592 | tf_op jit(solution)/shard_map/all_gather | solution.py:30
  11.8 17.0 %all-to-all-start = ((f32[8,16,128]{2,1,0:T(8,128)}), f32[8,16,128]{2,1,0:T(8,128)S(1)}, u32[]{:S(2)}, u32[]{:S(2)}) async-start(f32[8,16,128]{2,1,0:T(8,128)} %copy.25), calls=%async_computation | async-start | bytes 131072 | tf_op jit(solution)/shard_map/all_to_all | solution.py:47
  74.4 55.3 %all-to-all-start.1 = ((bf16[8,80,2048]{2,1,0:T(8,128)(2,1)}), bf16[8,80,2048]{2,1,0:T(8,128)(2,1)}, u32[]{:S(2)}, u32[]{:S(2)}) async-start(bf16[8,80,2048]{2,1,0:T(8,128)(2,1)} %bitcast.73), calls=%async_computation.1 | async-start | bytes 5242880 | tf_op jit(solution)/shard_map/all_to_all | solution.py:58
  129.7 37.2 %all-to-all-start.4 = ((bf16[8,80,2048]{2,1,0:T(8,128)(2,1)}), bf16[8,80,2048]{2,1,0:T(8,128)(2,1)}, u32[]{:S(2)}, u32[]{:S(2)}) async-start(bf16[8,80,2048]{2,1,0:T(8,128)(2,1)} %bitcast.74), calls=%async_computation.4 | async-start | bytes 5242880 | tf_op jit(solution)/shard_map/all_to_all | solution.py:58
  134.1 172.6 %reduce-scatter.4.cloned.1.call-start = ((), (), s32[]{:S(2)}) async-start(), calls=%async_computation.10 | async-start | bytes 3932160 | tf_op jit(solution)/shard_map/reduce_scatter | solution.py:94
  134.3 6.3 %copy-start.2 = (bf16[1,2048,768]{2,1,0:T(8,128)(2,1)S(1)}, bf16[1,2048,768]{2,1,0:T(8,128)(2,1)}, u32[]{:S(2)}) copy-start(bf16[1,2048,768]{2,1,0:T(8,128)(2,1)} %param.13) | copy-start | bytes 9437188
  139.3 1.3 copy-start.4
  166.9 5.5 %copy-start.5 = (f32[640,768]{1,0:T(8,128)S(1)}, f32[640,768]{1,0:T(8,128)}, u32[]{:S(2)}) copy-start(f32[640,768]{1,0:T(8,128)} %copy-done.4) | copy-start | bytes 5898244
  166.9 5.5 %copy-start.7 = (f32[640,768]{1,0:T(8,128)S(1)}, f32[640,768]{1,0:T(8,128)}, u32[]{:S(2)}) copy-start(f32[640,768]{1,0:T(8,128)} %get-tuple-element.7) | copy-start | bytes 5898244
  171.0 1.4 copy-start.6
  178.8 127.9 %reduce-scatter.6.cloned.1.call-start = ((), (), s32[]{:S(2)}) async-start(), calls=%async_computation.11 | async-start | bytes 3932160 | tf_op jit(solution)/shard_map/reduce_scatter | solution.py:94
  191.7 37.2 %all-to-all-start.2 = ((bf16[8,80,2048]{2,1,0:T(8,128)(2,1)}), bf16[8,80,2048]{2,1,0:T(8,128)(2,1)}, u32[]{:S(2)}, u32[]{:S(2)}) async-start(bf16[8,80,2048]{2,1,0:T(8,128)(2,1)} %bitcast.71), calls=%async_computation.2 | async-start | bytes 5242880 | tf_op jit(solution)/shard_map/all_to_all | solution.py:58
  196.1 110.6 %reduce-scatter.8.cloned.1.call-start = ((), (), s32[]{:S(2)}) async-start(), calls=%async_computation.12 | async-start | bytes 3932160 | tf_op jit(solution)/shard_map/reduce_scatter | solution.py:94
  196.1 2.3 copy-start.3
  234.2 66.9 %all-to-all-start.3 = ((bf16[8,80,2048]{2,1,0:T(8,128)(2,1)}), bf16[8,80,2048]{2,1,0:T(8,128)(2,1)}, u32[]{:S(2)}, u32[]{:S(2)}) async-start(bf16[8,80,2048]{2,1,0:T(8,128)(2,1)} %bitcast.72), calls=%async_computation.3 | async-start | bytes 5242880 | tf_op jit(solution)/shard_map/all_to_all | solution.py:79
  240.3 63.3 %copy-start.1 = (bf16[640,128]{1,0:T(8,128)(2,1)S(1)}, bf16[640,128]{1,0:T(8,128)(2,1)}, u32[]{:S(2)}) copy-start(bf16[640,128]{1,0:T(8,128)(2,1)} %convert_element_type.99) | copy-start | bytes 491524
Sparse Core Ops, SparseCore 0:
  9.8 57.7 all-gather.2
  69.4 53.3 all-gather.4
  178.9 35.6 reduce-scatter.3
  217.6 40.5 reduce-scatter.5
  261.1 40.5 reduce-scatter.7
where the time goes:
time: 314 us; the launch traced here: 313 us
  waiting for transfers between devices  195 us (62%)
  matrix products  66.3 us (21%)
  starting transfers between devices  26.7 us (9%)
  between operations  14 us (4%)
  other arithmetic  6.22 us (2%)
  local copies, waits for them, and re-layouts  5 us (2%)
    dot_general x16, matrix products, dot(): return lax.dot_general(a, b, (dims, ((), ())), preferred_element_type=F32)  66.3 us
    all_to_all x1, waiting for transfers between devices, local(): home = lax.all_to_all(returned, Z, 0, 0, tiled=True).reshape(rows, width)  60.8 us
    all_gather x1, waiting for transfers between devices, local(): all_grads = lax.all_gather(out_grad, Z, axis=0, tiled=True)  43.5 us
    all_to_all x3, waiting for transfers between devices, local(): lax.all_to_all(a.reshape(peers, block, width), (Y, C), 0, 0, tiled=True)  43.4 us
    all_gather x1, waiting for transfers between devices, local(): all_tokens = lax.all_gather(tokens, Z, axis=0, tiled=True)  37.5 us
    all_to_all x3, starting transfers between devices, local(): lax.all_to_all(a.reshape(peers, block, width), (Y, C), 0, 0, tiled=True)  13.2 us
    all_to_all x1, starting transfers between devices, local(): lax.all_to_all(jnp.concatenate([rank_z, weight_z], axis=1), Z, 0, 0, tile...  8.47 us
    all_to_all x1, waiting for transfers between devices, local(): lax.all_to_all(jnp.concatenate([rank_z, weight_z], axis=1), Z, 0, 0, tile...  8.4 us
  transfers between devices with their start and end apart: 10, of which 6 were waited for; matrix products, arithmetic and copies ran while one was open for 21% of the time, Pallas kernels for 0%

commit v1 on v0

v1 whole, which is shorter than its diff:
```python
import functools

import jax
import jax.numpy as jnp
from jax import lax
from jax.experimental import pallas as pl
from jax.experimental.pallas import tpu as pltpu
from jax.sharding import Mesh
from jax.sharding import PartitionSpec as P

Y, Z, C = "expert_y", "expert_z", "expert_c"
EXPERT = (Y, Z, C)
DP_EXPERT = ("dp",) + EXPERT
F32, BF16, I32 = jnp.float32, jnp.bfloat16, jnp.int32
LANES = 256
WIDE = 512


def dot(a, b, dims=((1,), (0,))):
    return lax.dot_general(a, b, (dims, ((), ())), preferred_element_type=F32)


def turn(a, axis, step):
    n = lax.axis_size(axis)
    return lax.ppermute(a, axis, [(i, (i + step) % n) for i in range(n)])


def swap(a):
    peers = lax.axis_size((Y, C))
    return lax.all_to_all(a.reshape(peers, -1, a.shape[1]), (Y, C), 0, 0, tiled=True).reshape(a.shape)


def params():
    return pltpu.CompilerParams(vmem_limit_bytes=56 * 2**20)


def cost(flops, moved):
    return pl.CostEstimate(flops=flops, bytes_accessed=moved, transcendentals=0)


def whole():
    return pl.BlockSpec(memory_space=pltpu.VMEM)


def smem():
    return pl.BlockSpec(memory_space=pltpu.SMEM)


def anywhere():
    return pl.BlockSpec(memory_space=pl.ANY)


def fixed(a):
    return pl.BlockSpec(a.shape, lambda n: (0,) * a.ndim)


def columns(a, wide):
    return pl.BlockSpec((a.shape[0], wide), lambda n: (0, n))


def start_loads(pairs, sems):
    loads = [pltpu.make_async_copy(src, dst, sems.at[i]) for i, (src, dst) in enumerate(pairs)]
    for load in loads:
        load.start()
    return loads


def pick_kernel(pick, *refs):
    picked = dot(pick[...], refs[-2][...])
    refs[-1][...] = (refs[0][...] * picked if len(refs) == 3 else picked).astype(BF16)


def pick_rows(pick, weight, tokens):
    rows, count = pick.shape
    out = jax.ShapeDtypeStruct((rows, tokens.shape[1]), BF16)
    return pl.pallas_call(
        pick_kernel,
        grid=(tokens.shape[1] // WIDE,),
        out_shape=out,
        in_specs=[fixed(pick)] + [fixed(w) for w in weight] + [columns(tokens, WIDE)],
        out_specs=columns(out, WIDE),
        compiler_params=params(),
        cost_estimate=cost(2 * pick.size * tokens.shape[1], 2 * (pick.size + tokens.size + out.size)),
    )(pick, *weight, tokens)


def terms_kernel(pick, weight, rows, out):
    held = (weight[...] * rows[...].astype(F32)).astype(BF16)
    out[...] = dot(pick[...], held).astype(BF16)


def token_terms(pick, weight, rows):
    out = jax.ShapeDtypeStruct((pick.shape[0], rows.shape[1]), BF16)
    return pl.pallas_call(
        terms_kernel,
        grid=(rows.shape[1] // WIDE,),
        out_shape=out,
        in_specs=[fixed(pick), fixed(weight), columns(rows, WIDE)],
        out_specs=columns(out, WIDE),
        compiler_params=params(),
        cost_estimate=cost(2 * pick.size * rows.shape[1], 2 * (pick.size + rows.size + out.size)),
    )(pick, weight, rows)


def hidden_kernel(rows_hbm, gate_hbm, up_hbm, hidden_ref, slope_ref, silu_ref, rows_ref, gate_w, up_w, sems):
    loads = start_loads(((rows_hbm, rows_ref), (gate_hbm, gate_w), (up_hbm, up_w)), sems)
    loads[0].wait()
    loads[1].wait()
    for n in range(0, hidden_ref.shape[1], LANES):
        cols = slice(n, n + LANES)
        gate = dot(rows_ref[...], gate_w[:, cols])
        if n == 0:
            loads[2].wait()
        up = dot(rows_ref[...], up_w[:, cols])
        sigma = jax.nn.sigmoid(gate)
        silu = gate * sigma
        silu_ref[:, cols] = silu
        slope_ref[:, cols] = up * (sigma * (1.0 + gate * (1.0 - sigma)))
        hidden_ref[:, cols] = (silu * up).astype(BF16)


def hidden_units(rows, w_gate, w_up):
    count = rows.shape[0]
    width, ff = w_gate.shape
    args = (rows, w_gate, w_up)
    return pl.pallas_call(
        hidden_kernel,
        out_shape=[jax.ShapeDtypeStruct((count, ff), kind) for kind in (BF16, F32, F32)],
        in_specs=[anywhere()] * 3,
        out_specs=[whole()] * 3,
        scratch_shapes=[pltpu.VMEM(a.shape, BF16) for a in args] + [pltpu.SemaphoreType.DMA((3,))],
        compiler_params=params(),
        cost_estimate=cost(4 * count * width * ff, 4 * width * ff + 2 * count * (width + 5 * ff)),
    )(*args)


def outputs_kernel(rows_ref, hidden_ref, down_w, out, rows_t, hidden_t):
    for n in range(0, out.shape[1], LANES):
        cols = slice(n, n + LANES)
        out[:, cols] = dot(hidden_ref[...], down_w[:, cols]).astype(BF16)
        rows_t[cols, :] = rows_ref[:, cols].T
    hidden_t[...] = hidden_ref[...].T


def outputs(rows, hidden, w_down):
    count, ff = hidden.shape
    width = w_down.shape[1]
    return pl.pallas_call(
        outputs_kernel,
        out_shape=[jax.ShapeDtypeStruct(shape, BF16) for shape in ((count, width), (width, count), (ff, count))],
        in_specs=[whole()] * 3,
        out_specs=[whole()] * 3,
        compiler_params=params(),
        cost_estimate=cost(2 * count * width * ff, 2 * width * (ff + 3 * count)),
    )(rows, hidden, w_down)


def down_kernel(hidden_t, outs, down):
    part = down.shape[2]
    for d in range(down.shape[0]):
        down[d] = dot(hidden_t[...], outs[:, d * part : (d + 1) * part]).astype(BF16)


def down_terms(hidden_t, outs, ndp):
    ff, count = hidden_t.shape
    width = outs.shape[1]
    return pl.pallas_call(
        down_kernel,
        out_shape=jax.ShapeDtypeStruct((ndp, ff, width // ndp), BF16),
        in_specs=[whole()] * 2,
        out_specs=whole(),
        compiler_params=params(),
        cost_estimate=cost(2 * count * ff * width, 2 * (count + ff) * width),
    )(hidden_t, outs)


def store_halves(a, b, cols, value):
    half = a.shape[0]
    a[:, cols] = value[:half]
    b[:, cols] = value[half:]


def share_columns(at, part):
    return pl.ds(pl.multiple_of(at * part, part), part)


def gate_up_share(mine, back_ref, store):
    for n in range(0, back_ref.shape[1], LANES):
        cols = slice(n, n + LANES)
        store(cols, dot(mine, back_ref[:, cols]).astype(BF16))


def backward_kernel(part, to, *refs):
    hbm, (far_a, far_b, back_ref) = refs[:5], refs[5:8]
    sems, held = refs[-1], refs[8:-1]
    loads = start_loads(tuple(zip(hbm, held)), sems)
    outr_ref, down_t, slope_ref, silu_ref, rows_t = held
    ff = down_t.shape[1]
    for load in loads[:4]:
        load.wait()
    for n in range(0, ff, LANES):
        cols = slice(n, n + LANES)
        hidden_grad = dot(outr_ref[...], down_t[:, cols])
        back_ref[:, cols] = (hidden_grad * slope_ref[:, cols]).astype(BF16)
        back_ref[:, ff + n : ff + n + LANES] = (hidden_grad * silu_ref[:, cols]).astype(BF16)
    loads[4].wait()
    gate_up_share(rows_t[share_columns(to[2], part), :], back_ref, functools.partial(store_halves, far_a, far_b))


def backward(to, outr, down_t, slope, silu, rows_t, ndp):
    count, width = outr.shape
    ff = down_t.shape[1]
    part = width // ndp
    full = lambda shape: jax.ShapeDtypeStruct(shape, BF16)
    piece = full((part // 2, 2 * ff))
    args = (outr, down_t, slope, silu, rows_t)
    return pl.pallas_call(
        functools.partial(backward_kernel, part),
        out_shape=[piece, piece, full((count, 2 * ff))],
        in_specs=[smem()] + [anywhere()] * len(args),
        out_specs=[whole()] * 3,
        scratch_shapes=[pltpu.VMEM(a.shape, a.dtype) for a in args] + [pltpu.SemaphoreType.DMA((len(args),))],
        compiler_params=params(),
        cost_estimate=cost(2 * count * width * ff + 4 * count * part * ff, 2 * width * ff + 10 * count * width),
    )(to, *args)


def shares_kernel(part, to, rows_t, back_ref, right_a, right_b, left_a, left_b, me):
    def own(cols, value):
        me[:, cols] = value

    stores = [functools.partial(store_halves, right_a, right_b), functools.partial(store_halves, left_a, left_b), own]
    for k, store in zip((1, 3, 0), stores):
        gate_up_share(rows_t[share_columns(to[k], part), :], back_ref, store)


def shares(to, rows_t, back, ndp):
    count, wide = back.shape
    part = rows_t.shape[0] // ndp
    half = jax.ShapeDtypeStruct((part // 2, wide), BF16)
    return pl.pallas_call(
        functools.partial(shares_kernel, part),
        out_shape=[half] * 4 + [jax.ShapeDtypeStruct((part, wide), BF16)],
        in_specs=[smem()] + [whole()] * 2,
        out_specs=[whole()] * 5,
        compiler_params=params(),
        cost_estimate=cost(6 * count * part * wide, 2 * (rows_t.size + back.size + 3 * part * wide)),
    )(to, rows_t, back)


def over_ring(far_a, far_b, right_a, right_b, left_a, left_b, axis):
    add = lambda a, b: (a.astype(F32) + b.astype(F32)).astype(BF16)
    from_left, from_right = turn(far_a, axis, 1), turn(far_b, axis, -1)
    left_high, right_low = turn(right_b, axis, 1), turn(left_a, axis, -1)
    left_low = turn(add(right_a, from_left), axis, 1)
    right_high = turn(add(left_b, from_right), axis, -1)
    return left_low, left_high, right_low, right_high


def total_kernel(me, left_low, left_high, right_low, right_high, *outs):
    half = left_low.shape[0]
    wide = outs[0].shape[1]
    for i, (left, right) in enumerate(((left_low, right_low), (left_high, right_high))):
        span = slice(i * half, (i + 1) * half)
        for k, out in enumerate(outs):
            cols = slice(k * wide, (k + 1) * wide)
            total = me[span, cols].astype(F32) + left[:, cols].astype(F32) + right[:, cols].astype(F32)
            out[span, :] = total.astype(BF16)


def totals(me, others, count):
    rows, wide = me.shape
    return pl.pallas_call(
        total_kernel,
        out_shape=[jax.ShapeDtypeStruct((rows, wide // count), BF16)] * count,
        in_specs=[whole()] * 5,
        out_specs=[whole()] * count,
        compiler_params=params(),
        cost_estimate=cost(3 * me.size, 8 * me.size),
    )(me, *others)


def local(tokens, expert_ids, probs, trade, gate_weight, up_weight, down_weight, out_grad):
    tok_count, width = tokens.shape
    top_count = expert_ids.shape[1]
    ny, nz, nc = (lax.axis_size(a) for a in EXPERT)
    peers = ny * nc
    halfway = ny * nz * nc // 2
    cap = 5 * tok_count * top_count // (4 * ny * nz * nc)
    block = nz * cap
    rows = peers * block
    ndp = lax.axis_size("dp")
    mz, here = lax.axis_index(Z), lax.axis_index("dp")
    after = lambda arrays, *first: lax.optimization_barrier((arrays,) + first)[0]

    all_tokens = lax.all_gather(tokens, Z, axis=0, tiled=True)

    raw = jnp.concatenate([expert_ids.astype(F32).T, probs.T], axis=0)
    near = jnp.stack([raw] + [turn(raw, Z, -k) for k in range(1, nz)])
    info = jnp.roll(near, mz, axis=0)

    p = jnp.arange(peers, dtype=I32)
    device = p // nc * (nz * nc) + mz * nc + p % nc
    numbers = jnp.arange(halfway, dtype=I32)
    traded = jnp.any(((device % halfway)[:, None] == numbers) & (trade == 1), axis=1)
    expert = jnp.where(traded, jnp.bitwise_xor(device, halfway), device).astype(F32)
    hits = info[None, :, :top_count] == expert[:, None, None, None]
    named = jnp.any(hits, axis=2)
    weight = jnp.sum(jnp.where(hits, info[None, :, top_count:], 0.0), axis=2)
    before = (
        lax.broadcasted_iota(I32, (tok_count, tok_count), 0)
        < lax.broadcasted_iota(I32, (tok_count, tok_count), 1)
    ).astype(BF16)
    rank = dot(named.astype(BF16).reshape(peers * nz, tok_count), before).reshape(named.shape)
    row_of = jnp.where(named, rank + (jnp.arange(nz, dtype=F32) * cap)[:, None], -1.0)
    flat = lambda a: a.reshape(peers, 1, nz * tok_count)
    match = flat(row_of) == jnp.arange(block, dtype=F32)[None, :, None]
    pick = match.astype(BF16).reshape(rows, nz * tok_count)
    row_weight = jnp.sum(jnp.where(match, flat(weight), 0.0), axis=2).reshape(rows, 1)
    spread = pick.T
    w_down = down_weight[0]
    down_t = w_down.T
    all_grads = lax.all_gather(after(out_grad, pick, row_weight, spread, down_t), Z, axis=0, tiled=True)

    w_gate, w_up = gate_weight[0], up_weight[0]
    expert_rows = swap(pick_rows(pick, [], all_tokens))
    hidden, slope, silu = hidden_units(expert_rows, w_gate, w_up)
    picked = pick_rows(pick, [row_weight], after(all_grads, hidden))
    out_rows = swap(picked)
    expert_out, rows_t, hidden_t = outputs(expert_rows, after(hidden, picked), w_down)
    returned = swap(expert_out)

    to = (here + jnp.arange(ndp, dtype=I32)) % ndp
    down = down_terms(hidden_t, out_rows, ndp)
    down_part = lax.psum_scatter(down, "dp", scatter_dimension=0, tiled=True)
    *far, back = backward(to, after(out_rows, down), down_t, slope, silu, rows_t, ndp)
    *near, me = shares(to, rows_t, back, ndp)
    gate_part, up_part = totals(me, over_ring(*far, *near, "dp"), 2)

    returned = after(returned, near)
    combined = lax.psum_scatter(token_terms(spread, row_weight, returned), Z, scatter_dimension=0, tiled=True)
    return combined, gate_part[None], up_part[None], down_part


def solution(mesh):
    finer = Mesh(mesh.devices.reshape(mesh.shape["dp"], 4, 8, 2), DP_EXPERT)
    rows = P(DP_EXPERT, None)
    stored = P(EXPERT, None, None)
    return jax.shard_map(
        local,
        mesh=finer,
        in_specs=(rows, rows, rows, P(), stored, stored, stored, rows),
        out_specs=(rows, P(EXPERT, "dp", None), P(EXPERT, "dp", None), P(EXPERT, None, "dp")),
        check_vma=False,
    )
```

time: 314 us -> 287 us (0.914)
  Pallas kernels: 0 us -> 68.5 us
  matrix products: 66.3 us -> 0.1 us
  waiting for transfers between devices: 195 us -> 143 us
  local copies, waits for them, and re-layouts: 5 us -> 17.8 us
  starting transfers between devices: 26.7 us -> 35.7 us
    pallas_call x0 -> x9, Pallas kernels: none -> 68.5 us  [the longest x2 13.4 us: pick_rows(): pl.pallas_call(pick_kernel, grid=(tokens.shape[1] // WIDE,), out_shape=ou...]
    dot_general x16 -> x1, matrix products: 66.3 us -> 0.1 us  [dot(): return lax.dot_general(a, b, (dims, ((), ())), preferred_element_type=F32)]
    ppermute x0 -> x13, waiting for transfers between devices: none -> 54.8 us  [turn(): return lax.ppermute(a, axis, [(i, (i + step) % n) for i in range(n)])]
    all_gather x1, waiting for transfers between devices: 43.5 us -> 0.02 us  [local(): lax.all_gather(after(out_grad, pick, row_weight, spread, down_t), Z, axis...]
    all_to_all x5 -> x3, waiting for transfers between devices: 113 us -> 69.7 us  [swap(): lax.all_to_all(a.reshape(peers, -1, a.shape[1]), (Y, C), 0, 0, tiled=True)]
    ppermute x0 -> x13, starting transfers between devices: none -> 23.7 us  [turn(): return lax.ppermute(a, axis, [(i, (i + step) % n) for i in range(n)])]
    all_gather x1, waiting for transfers between devices: 37.5 us -> 17.5 us  [local(): all_tokens = lax.all_gather(tokens, Z, axis=0, tiled=True)]
    all_to_all x5 -> x3, starting transfers between devices: 26.1 us -> 11.6 us  [swap(): lax.all_to_all(a.reshape(peers, -1, a.shape[1]), (Y, C), 0, 0, tiled=True)]
  transfers between devices with their start and end apart: 10 -> 20, of which waited for: 6 -> 11; matrix products, arithmetic and copies ran while one was open for 21% -> 7% of each run, Pallas kernels for 0% -> 19%
where the time goes in v1:
time: 287 us; the launch traced here: 286 us
  waiting for transfers between devices  143 us (50%)
  Pallas kernels  68.5 us (24%)
  starting transfers between devices  35.7 us (12%)
  local copies, waits for them, and re-layouts  17.8 us (6%)
  between operations  14.1 us (5%)
  other arithmetic  7.02 us (2%)
    all_to_all x3, waiting for transfers between devices, swap(): lax.all_to_all(a.reshape(peers, -1, a.shape[1]), (Y, C), 0, 0, tiled=True)  69.7 us
    ppermute x13, waiting for transfers between devices, turn(): return lax.ppermute(a, axis, [(i, (i + step) % n) for i in range(n)])  54.8 us
    ppermute x13, starting transfers between devices, turn(): return lax.ppermute(a, axis, [(i, (i + step) % n) for i in range(n)])  23.7 us
    all_gather x1, waiting for transfers between devices, local(): all_tokens = lax.all_gather(tokens, Z, axis=0, tiled=True)  17.5 us
    pallas_call x2, Pallas kernels, pick_rows(): pl.pallas_call(pick_kernel, grid=(tokens.shape[1] // WIDE,), out_shape=ou...  13.4 us
    pallas_call x1, Pallas kernels, backward(): pl.pallas_call(functools.partial(backward_kernel, part), out_shape=[piece...  11.9 us
    all_to_all x3, starting transfers between devices, swap(): lax.all_to_all(a.reshape(peers, -1, a.shape[1]), (Y, C), 0, 0, tiled=True)  11.6 us
    pallas_call x1, Pallas kernels, hidden_units(): pl.pallas_call(hidden_kernel, out_shape=[jax.ShapeDtypeStruct((count, ff)...  10.8 us
  transfers between devices with their start and end apart: 20, of which 11 were waited for; matrix products, arithmetic and copies ran while one was open for 7% of the time, Pallas kernels for 19%

profile of v1, /device:TPU:6, one launch (start us, length us, event | category | flops | bytes accessed | tf_op | source)
XLA Modules:
  0.0 285.9 jit_solution(4489299078645531135)
XLA Ops:
  9.3 3.3 %collective-permute-start.5 = (f32[8,128]{1,0:T(8,128)S(1)}, f32[8,128]{1,0:T(8,128)S(1)}, u32[]{:S(2)}, u32[]{:S(2)}) collective-permute-start(f32[8,128]{1,0:T(8,128)S(1)} %pad_maximum_fusion), channel_id=1, source_target_pairs={{0,4},{2,6},{4,8},{6,10},{8,12},{10,14},{12,0},{14,2},{1,5},{3,7},... | collective-permute-start | bytes 12296 | tf_op jit(solution)/shard_map/ppermute | solution.py:25
  12.6 4.9 %collective-permute-start.4 = (f32[8,128]{1,0:T(8,128)S(1)}, f32[8,128]{1,0:T(8,128)S(1)}, u32[]{:S(2)}, u32[]{:S(2)}) collective-permute-start(f32[8,128]{1,0:T(8,128)S(1)} %pad_maximum_fusion), channel_id=1, source_target_pairs={{0,6},{2,8},{4,10},{6,12},{8,14},{10,0},{12,2},{14,4},{1,7},{3,9},... | collective-permute-start | bytes 12296 | tf_op jit(solution)/shard_map/ppermute | solution.py:25
  18.5 4.5 %collective-permute-start.2 = (f32[8,128]{1,0:T(8,128)S(1)}, f32[8,128]{1,0:T(8,128)S(1)}, u32[]{:S(2)}, u32[]{:S(2)}) collective-permute-start(f32[8,128]{1,0:T(8,128)S(1)} %pad_maximum_fusion), channel_id=1, source_target_pairs={{0,10},{2,12},{4,14},{6,0},{8,2},{10,4},{12,6},{14,8},{1,11},{3,13... | collective-permute-start | bytes 12296 | tf_op jit(solution)/shard_map/ppermute | solution.py:25
  25.7 4.7 %copy.28 = bf16[1,768,2048]{1,2,0:T(8,128)(2,1)} copy(bf16[1,768,2048]{2,1,0:T(8,128)(2,1)} %param.14) | data formatting | bytes 6291456 | tf_op args[6]
  30.4 1.7 collective-permute-start.1
  32.1 2.9 %collective-permute-done.1 = f32[8,128]{1,0:T(8,128)S(1)} collective-permute-done((f32[8,128]{1,0:T(8,128)S(1)}, f32[8,128]{1,0:T(8,128)S(1)}, u32[]{:S(2)}, u32[]{:S(2)}) %collective-permute-start.1) | collective-permute-done | bytes 4128 | tf_op jit(solution)/shard_map/ppermute | solution.py:25
  36.1 4.0 %collective-permute-done.6 = f32[8,128]{1,0:T(8,128)S(1)} collective-permute-done((f32[8,128]{1,0:T(8,128)S(1)}, f32[8,128]{1,0:T(8,128)S(1)}, u32[]{:S(2)}, u32[]{:S(2)}) %collective-permute-start.6) | collective-permute-done | bytes 4128 | tf_op jit(solution)/shard_map/ppermute | solution.py:25
  41.0 1.9 eq.75
  42.9 2.2 copy.25
  47.7 2.5 copy.27.pick
  50.2 17.5 %all-gather.3.cloned.1.call-done.refs_0_ = bf16[1024,2048]{1,0:T(8,128)(2,1)} async-done(((bf16[128,2048]{1,0:T(8,128)(2,1)}), bf16[1024,2048]{1,0:T(8,128)(2,1)}) %all-gather.3.cloned.1.call-update) | async-done | bytes 4194320 | tf_op jit(solution)/shard_map/all_gather | solution.py:296
  67.6 6.7 %shard_map.111 = bf16[640,2048]{1,0:T(8,128)(2,1)} custom-call(bf16[640,1024]{1,0:T(8,128)(2,1)} %copy.27.pick, bf16[1024,2048]{1,0:T(8,128)(2,1)} %all-gather.3.cloned.1.call-done.refs_0_), custom_call_target="tpu_custom_call" | custom-call | flops 2684354560 | bytes 8126464 | tf_op jit(solution)/shard_map/pallas_call | solution.py:76
  74.3 4.3 %all-to-all-start = ((bf16[8,80,2048]{2,1,0:T(8,128)(2,1)}), bf16[8,80,2048]{2,1,0:T(8,128)(2,1)S(1)}, u32[]{:S(2)}, u32[]{:S(2)}) async-start(bf16[8,80,2048]{2,1,0:T(8,128)(2,1)} %bitcast.64), calls=%async_computation | async-start | bytes 5242880 | tf_op jit(solution)/shard_map/all_to_all | solution.py:30
  79.5 31.9 %all-to-all-done = bf16[8,80,2048]{2,1,0:T(8,128)(2,1)S(1)} async-done(((bf16[8,80,2048]{2,1,0:T(8,128)(2,1)}), bf16[8,80,2048]{2,1,0:T(8,128)(2,1)S(1)}, u32[]{:S(2)}, u32[]{:S(2)}) %all-to-all-start) | async-done | bytes 2621472 | tf_op jit(solution)/shard_map/all_to_all | solution.py:30
  112.9 10.8 %shard_map.112 = (bf16[640,768]{1,0:T(8,128)(2,1)}, f32[640,768]{1,0:T(8,128)}, f32[640,768]{1,0:T(8,128)}) custom-call(bf16[640,2048]{1,0:T(8,128)(2,1)} %bitcast.61, bf16[2048,768]{1,0:T(8,128)(2,1)} %bitcast.69, bf16[2048,768]{1,0:T(8,128)(2,1)} %bitcast.70), custom_call_target="tpu_custom_call" | custom-call | flops 4026531840 | bytes 13828096 | tf_op jit(solution)/shard_map/pallas_call | solution.py:126
  123.7 6.7 %shard_map.113 = bf16[640,2048]{1,0:T(8,128)(2,1)} custom-call(bf16[640,1024]{1,0:T(8,128)(2,1)} %copy.27.pick, f32[640,1]{1,0:T(8,128)} %copy.32.refs_0_.weight, bf16[1024,2048]{1,0:T(8,128)(2,1)} %all-gather.5.cloned.1.call-done.refs_1_), custom_call_target="tpu_custom_call" | custom-call | flops 2684354560 | bytes 8126464 | tf_op jit(solution)/shard_map/pallas_call | solution.py:76
  130.4 3.6 %all-to-all-start.2 = ((bf16[8,80,2048]{2,1,0:T(8,128)(2,1)}), bf16[8,80,2048]{2,1,0:T(8,128)(2,1)S(1)}, u32[]{:S(2)}, u32[]{:S(2)}) async-start(bf16[8,80,2048]{2,1,0:T(8,128)(2,1)} %bitcast.63), calls=%async_computation.2 | async-start | bytes 5242880 | tf_op jit(solution)/shard_map/all_to_all | solution.py:30
  134.1 7.5 %shard_map.114 = (bf16[640,2048]{1,0:T(8,128)(2,1)}, bf16[2048,640]{1,0:T(8,128)(2,1)}, bf16[768,640]{1,0:T(8,128)(2,1)}) custom-call(bf16[640,2048]{1,0:T(8,128)(2,1)} %bitcast.62, bf16[640,768]{1,0:T(8,128)(2,1)} %get-tuple-element.28.hidden_ref, bf16[768,2048]{1,0:T(8,128)(2,1)} %bitcast.59), custom_call_target="tpu_custom_call" | custom-call | flops 2013265920 | bytes 11010048 | tf_op jit(solution)/shard_map/pallas_call | solution.py:148
  141.7 25.1 %all-to-all-done.2 = bf16[8,80,2048]{2,1,0:T(8,128)(2,1)S(1)} async-done(((bf16[8,80,2048]{2,1,0:T(8,128)(2,1)}), bf16[8,80,2048]{2,1,0:T(8,128)(2,1)S(1)}, u32[]{:S(2)}, u32[]{:S(2)}) %all-to-all-start.2) | async-done | bytes 2621472 | tf_op jit(solution)/shard_map/all_to_all | solution.py:30
  168.3 6.3 %shard_map.115 = bf16[4,768,512]{2,1,0:T(8,128)(2,1)} custom-call(bf16[768,640]{1,0:T(8,128)(2,1)} %get-tuple-element.31.hidden_t, bf16[640,2048]{1,0:T(8,128)(2,1)} %bitcast.57), custom_call_target="tpu_custom_call" | custom-call | flops 2013265920 | bytes 5767168 | tf_op jit(solution)/shard_map/pallas_call | solution.py:167
  174.7 3.6 %all-to-all-start.1 = ((bf16[8,80,2048]{2,1,0:T(8,128)(2,1)}), bf16[8,80,2048]{2,1,0:T(8,128)(2,1)S(1)}, u32[]{:S(2)}, u32[]{:S(2)}) async-start(bf16[8,80,2048]{2,1,0:T(8,128)(2,1)} %bitcast.20), calls=%async_computation.1 | async-start | bytes 5242880 | tf_op jit(solution)/shard_map/all_to_all | solution.py:30
  179.1 11.9 %shard_map.116 = (bf16[256,1536]{1,0:T(8,128)(2,1)}, bf16[256,1536]{1,0:T(8,128)(2,1)}, bf16[640,1536]{1,0:T(8,128)(2,1)}) custom-call(s32[4]{0:T(128)} %and_select_fusion.to, bf16[640,2048]{1,0:T(8,128)(2,1)} %bitcast.58, bf16[2048,768]{1,0:T(8,128)(2,1)} %bitcast.55, f32[640,768]{1,0:T(8,128)} %get-tuple-element.33.refs_2_, ...), custom_call_target="tpu_custom_call" | custom-call | flops 3019898880 | bytes 16252928 | tf_op jit(solution)/shard_map/pallas_call | solution.py:217
  191.0 7.4 %shard_map.117 = (bf16[256,1536]{1,0:T(8,128)(2,1)}, bf16[256,1536]{1,0:T(8,128)(2,1)}, bf16[256,1536]{1,0:T(8,128)(2,1)}, bf16[256,1536]{1,0:T(8,128)(2,1)}, bf16[512,1536]{1,0:T(8,128)(2,1)}) custom-call(s32[4]{0:T(128)} %and_select_fusion.to, bf16[2048,640]{1,0:T(8,128)(2,1)} %get-tuple-element.30.refs_4_.rows_t, bf16[640,1536]{1,0:T(8,128)(2,1)} %get-tuple-element.35.back_ref), custom_call_target="tpu_custom_call" | custom-call | flops 3019898880 | bytes 9306112 | tf_op jit(solution)/shard_map/pallas_call | solution.py:241
  198.4 12.7 %all-to-all-done.1 = bf16[8,80,2048]{2,1,0:T(8,128)(2,1)S(1)} async-done(((bf16[8,80,2048]{2,1,0:T(8,128)(2,1)}), bf16[8,80,2048]{2,1,0:T(8,128)(2,1)S(1)}, u32[]{:S(2)}, u32[]{:S(2)}) %all-to-all-start.1) | async-done | bytes 2621472 | tf_op jit(solution)/shard_map/all_to_all | solution.py:30
  212.5 7.4 %shard_map.118 = bf16[1024,2048]{1,0:T(8,128)(2,1)} custom-call(bf16[1024,640]{1,0:T(8,128)(2,1)} %fusion.14.pick, f32[640,1]{1,0:T(8,128)} %copy.32.refs_0_.weight, bf16[640,2048]{1,0:T(8,128)(2,1)} %bitcast.60), custom_call_target="tpu_custom_call" | custom-call | flops 2684354560 | bytes 8126464 | tf_op jit(solution)/shard_map/pallas_call | solution.py:94
  222.1 1.8 collective-permute-start.9
  224.1 16.6 %collective-permute-done.7 = bf16[256,1536]{1,0:T(8,128)(2,1)S(1)} collective-permute-done((bf16[256,1536]{1,0:T(8,128)(2,1)}, bf16[256,1536]{1,0:T(8,128)(2,1)S(1)}, u32[]{:S(2)}, u32[]{:S(2)}) %collective-permute-start.7) | collective-permute-done | bytes 786464 | tf_op jit(solution)/shard_map/ppermute | solution.py:25
  240.9 1.8 collective-permute-start.8
  243.3 14.3 %collective-permute-done.9.left_high = bf16[256,1536]{1,0:T(8,128)(2,1)S(1)} collective-permute-done((bf16[256,1536]{1,0:T(8,128)(2,1)S(1)}, bf16[256,1536]{1,0:T(8,128)(2,1)S(1)}, u32[]{:S(2)}, u32[]{:S(2)}) %collective-permute-start.9) | collective-permute-done | bytes 786464 | tf_op jit(solution)/shard_map/ppermute | solution.py:25
  257.6 1.8 collective-permute-done.10.right_low
  259.4 13.7 %collective-permute-done.8.left_low = bf16[256,1536]{1,0:T(8,128)(2,1)S(1)} collective-permute-done((bf16[256,1536]{1,0:T(8,128)(2,1)S(1)}, bf16[256,1536]{1,0:T(8,128)(2,1)S(1)}, u32[]{:S(2)}, u32[]{:S(2)}) %collective-permute-start.8) | collective-permute-done | bytes 786464 | tf_op jit(solution)/shard_map/ppermute | solution.py:25
  275.4 3.9 %shard_map.119 = (bf16[512,768]{1,0:T(8,128)(2,1)}, bf16[512,768]{1,0:T(8,128)(2,1)}) custom-call(bf16[512,1536]{1,0:T(8,128)(2,1)} %get-tuple-element.41.me, bf16[256,1536]{1,0:T(8,128)(2,1)} %copy-done.5, bf16[256,1536]{1,0:T(8,128)(2,1)} %copy-done.3, bf16[256,1536]{1,0:T(8,128)(2,1)} %copy-done.4, bf16[256,1536]{1,0:T(8,128)(2,1)} %copy-done.6), custom_call_target="tpu_custom_call" | custom-call | flops 2359296 | bytes 6291456 | tf_op jit(solution)/shard_map/pallas_call | solution.py:273
  (89 shorter events, 22.0 us)
Async XLA Ops:
  7.2 60.5 %all-gather.3.cloned.1.call-start = ((), (), s32[]{:S(2)}) async-start(), calls=%async_computation.5 | async-start | bytes 4718592 | tf_op jit(solution)/shard_map/all_gather | solution.py:296
  7.9 115.8 %all-gather.5.cloned.1.call-start = ((), (), s32[]{:S(2)}) async-start(), calls=%async_computation.6 | async-start | bytes 4718592 | tf_op jit(solution)/shard_map/all_gather | solution.py:323
  9.3 26.7 %collective-permute-start.5 = (f32[8,128]{1,0:T(8,128)S(1)}, f32[8,128]{1,0:T(8,128)S(1)}, u32[]{:S(2)}, u32[]{:S(2)}) collective-permute-start(f32[8,128]{1,0:T(8,128)S(1)} %pad_maximum_fusion), channel_id=1, source_target_pairs={{0,4},{2,6},{4,8},{6,10},{8,12},{10,14},{12,0},{14,2},{1,5},{3,7},... | collective-permute-start | bytes 12296 | tf_op jit(solution)/shard_map/ppermute | solution.py:25
  12.6 23.5 %collective-permute-start.4 = (f32[8,128]{1,0:T(8,128)S(1)}, f32[8,128]{1,0:T(8,128)S(1)}, u32[]{:S(2)}, u32[]{:S(2)}) collective-permute-start(f32[8,128]{1,0:T(8,128)S(1)} %pad_maximum_fusion), channel_id=1, source_target_pairs={{0,6},{2,8},{4,10},{6,12},{8,14},{10,0},{12,2},{14,4},{1,7},{3,9},... | collective-permute-start | bytes 12296 | tf_op jit(solution)/shard_map/ppermute | solution.py:25
  17.5 18.5 %collective-permute-start.3 = (f32[8,128]{1,0:T(8,128)S(1)}, f32[8,128]{1,0:T(8,128)S(1)}, u32[]{:S(2)}, u32[]{:S(2)}) collective-permute-start(f32[8,128]{1,0:T(8,128)S(1)} %pad_maximum_fusion), channel_id=1, source_target_pairs={{0,8},{2,10},{4,12},{6,14},{8,0},{10,2},{12,4},{14,6},{1,9},{3,11}... | collective-permute-start | bytes 12296 | tf_op jit(solution)/shard_map/ppermute | solution.py:25
  18.5 17.5 %collective-permute-start.2 = (f32[8,128]{1,0:T(8,128)S(1)}, f32[8,128]{1,0:T(8,128)S(1)}, u32[]{:S(2)}, u32[]{:S(2)}) collective-permute-start(f32[8,128]{1,0:T(8,128)S(1)} %pad_maximum_fusion), channel_id=1, source_target_pairs={{0,10},{2,12},{4,14},{6,0},{8,2},{10,4},{12,6},{14,8},{1,11},{3,13... | collective-permute-start | bytes 12296 | tf_op jit(solution)/shard_map/ppermute | solution.py:25
  23.0 7.4 %collective-permute-start = (f32[8,128]{1,0:T(8,128)S(1)}, f32[8,128]{1,0:T(8,128)S(1)}, u32[]{:S(2)}, u32[]{:S(2)}) collective-permute-start(f32[8,128]{1,0:T(8,128)S(1)} %pad_maximum_fusion), channel_id=1, source_target_pairs={{0,14},{2,0},{4,2},{6,4},{8,6},{10,8},{12,10},{14,12},{1,15},{3,1}... | collective-permute-start | bytes 12296 | tf_op jit(solution)/shard_map/ppermute | solution.py:25
  25.7 14.4 %copy-start.9 = (f32[128,4]{0,1:T(4,128)S(1)}, f32[128,4]{0,1:T(4,128)}, u32[]{:S(2)}) copy-start(f32[128,4]{0,1:T(4,128)} %param.10) | copy-start | bytes 6148
  30.4 4.6 %collective-permute-start.1 = (f32[8,128]{1,0:T(8,128)S(1)}, f32[8,128]{1,0:T(8,128)S(1)}, u32[]{:S(2)}, u32[]{:S(2)}) collective-permute-start(f32[8,128]{1,0:T(8,128)S(1)} %pad_maximum_fusion), channel_id=1, source_target_pairs={{0,12},{2,14},{4,0},{6,2},{8,4},{10,6},{12,8},{14,10},{1,13},{3,15... | collective-permute-start | bytes 12296 | tf_op jit(solution)/shard_map/ppermute | solution.py:25
  35.0 5.1 %collective-permute-start.6 = (f32[8,128]{1,0:T(8,128)S(1)}, f32[8,128]{1,0:T(8,128)S(1)}, u32[]{:S(2)}, u32[]{:S(2)}) collective-permute-start(f32[8,128]{1,0:T(8,128)S(1)} %pad_maximum_fusion), channel_id=1, source_target_pairs={{0,2},{2,4},{4,6},{6,8},{8,10},{10,12},{12,14},{14,0},{1,3},{3,5},... | collective-permute-start | bytes 12296 | tf_op jit(solution)/shard_map/ppermute | solution.py:25
  74.3 37.1 %all-to-all-start = ((bf16[8,80,2048]{2,1,0:T(8,128)(2,1)}), bf16[8,80,2048]{2,1,0:T(8,128)(2,1)S(1)}, u32[]{:S(2)}, u32[]{:S(2)}) async-start(bf16[8,80,2048]{2,1,0:T(8,128)(2,1)} %bitcast.64), calls=%async_computation | async-start | bytes 5242880 | tf_op jit(solution)/shard_map/all_to_all | solution.py:30
  111.4 1.5 copy-start.2
  130.4 36.4 %all-to-all-start.2 = ((bf16[8,80,2048]{2,1,0:T(8,128)(2,1)}), bf16[8,80,2048]{2,1,0:T(8,128)(2,1)S(1)}, u32[]{:S(2)}, u32[]{:S(2)}) async-start(bf16[8,80,2048]{2,1,0:T(8,128)(2,1)} %bitcast.63), calls=%async_computation.2 | async-start | bytes 5242880 | tf_op jit(solution)/shard_map/all_to_all | solution.py:30
  134.1 145.3 %reduce-scatter.5.cloned.1.call-start = ((), (), s32[]{:S(2)}) async-start(), calls=%async_computation.8 | async-start | bytes 3932160 | tf_op jit(solution)/shard_map/reduce_scatter | solution.py:335
  166.8 1.5 copy-start
  174.7 36.4 %all-to-all-start.1 = ((bf16[8,80,2048]{2,1,0:T(8,128)(2,1)}), bf16[8,80,2048]{2,1,0:T(8,128)(2,1)S(1)}, u32[]{:S(2)}, u32[]{:S(2)}) async-start(bf16[8,80,2048]{2,1,0:T(8,128)(2,1)} %bitcast.20), calls=%async_computation.1 | async-start | bytes 5242880 | tf_op jit(solution)/shard_map/all_to_all | solution.py:30
  178.3 101.0 %reduce-scatter.3.cloned.1.call-start = ((), (), s32[]{:S(2)}) async-start(), calls=%async_computation.7 | async-start | bytes 4718592 | tf_op jit(solution)/shard_map/reduce_scatter | solution.py:341
  211.0 1.5 copy-start.1
  219.9 2.1 copy-start.11
  219.9 3.9 %copy-start.10 = (bf16[256,1536]{1,0:T(8,128)(2,1)S(1)}, bf16[256,1536]{1,0:T(8,128)(2,1)}, u32[]{:S(2)}) copy-start(bf16[256,1536]{1,0:T(8,128)(2,1)} %get-tuple-element.38) | copy-start | bytes 2359300
  219.9 20.8 %copy-start.8 = (bf16[256,1536]{1,0:T(8,128)(2,1)S(1)}, bf16[256,1536]{1,0:T(8,128)(2,1)}, u32[]{:S(2)}) copy-start(bf16[256,1536]{1,0:T(8,128)(2,1)} %get-tuple-element.36) | copy-start | bytes 2359300
  220.0 22.8 %copy-start.7 = (bf16[256,1536]{1,0:T(8,128)(2,1)S(1)}, bf16[256,1536]{1,0:T(8,128)(2,1)}, u32[]{:S(2)}) copy-start(bf16[256,1536]{1,0:T(8,128)(2,1)} %get-tuple-element.39) | copy-start | bytes 2359300
  220.0 20.7 %collective-permute-start.7 = (bf16[256,1536]{1,0:T(8,128)(2,1)}, bf16[256,1536]{1,0:T(8,128)(2,1)S(1)}, u32[]{:S(2)}, u32[]{:S(2)}) collective-permute-start(bf16[256,1536]{1,0:T(8,128)(2,1)} %get-tuple-element.42), channel_id=1, source_target_pairs={{0,64},{64,128},{128,192},{192,0},{1,65},{65,129},{129,193},{193,1... | collective-permute-start | bytes 2359304 | tf_op jit(solution)/shard_map/ppermute | solution.py:25
  220.6 22.2 %collective-permute-start.11 = (bf16[256,1536]{1,0:T(8,128)(2,1)}, bf16[256,1536]{1,0:T(8,128)(2,1)S(1)}, u32[]{:S(2)}, u32[]{:S(2)}) collective-permute-start(bf16[256,1536]{1,0:T(8,128)(2,1)} %get-tuple-element.43), channel_id=1, source_target_pairs={{0,192},{64,0},{128,64},{192,128},{1,193},{65,1},{129,65},{193,129... | collective-permute-start | bytes 2359304 | tf_op jit(solution)/shard_map/ppermute | solution.py:25
  222.1 35.5 %collective-permute-start.9 = (bf16[256,1536]{1,0:T(8,128)(2,1)S(1)}, bf16[256,1536]{1,0:T(8,128)(2,1)S(1)}, u32[]{:S(2)}, u32[]{:S(2)}) collective-permute-start(bf16[256,1536]{1,0:T(8,128)(2,1)S(1)} %copy-done.11), channel_id=1, source_target_pairs={{0,64},{64,128},{128,192},{192,0},{1,65},{65,129},{129,193},{193,1... | collective-permute-start | bytes 2359304 | tf_op jit(solution)/shard_map/ppermute | solution.py:25
  223.9 35.5 %collective-permute-start.10 = (bf16[256,1536]{1,0:T(8,128)(2,1)S(1)}, bf16[256,1536]{1,0:T(8,128)(2,1)S(1)}, u32[]{:S(2)}, u32[]{:S(2)}) collective-permute-start(bf16[256,1536]{1,0:T(8,128)(2,1)S(1)} %copy-done.10), channel_id=1, source_target_pairs={{0,192},{64,0},{128,64},{192,128},{1,193},{65,1},{129,65},{193,129... | collective-permute-start | bytes 2359304 | tf_op jit(solution)/shard_map/ppermute | solution.py:25
  240.9 32.1 %collective-permute-start.8 = (bf16[256,1536]{1,0:T(8,128)(2,1)S(1)}, bf16[256,1536]{1,0:T(8,128)(2,1)S(1)}, u32[]{:S(2)}, u32[]{:S(2)}) collective-permute-start(bf16[256,1536]{1,0:T(8,128)(2,1)S(1)} %add_convert_fusion.1), channel_id=1, source_target_pairs={{0,64},{64,128},{128,192},{192,0},{1,65},{65,129},{129,193},{193,1... | collective-permute-start | bytes 2359304 | tf_op jit(solution)/shard_map/ppermute | solution.py:25
  243.0 31.6 %collective-permute-start.12 = (bf16[256,1536]{1,0:T(8,128)(2,1)S(1)}, bf16[256,1536]{1,0:T(8,128)(2,1)S(1)}, u32[]{:S(2)}, u32[]{:S(2)}) collective-permute-start(bf16[256,1536]{1,0:T(8,128)(2,1)S(1)} %add_convert_fusion), channel_id=1, source_target_pairs={{0,192},{64,0},{128,64},{192,128},{1,193},{65,1},{129,65},{193,129... | collective-permute-start | bytes 2359304 | tf_op jit(solution)/shard_map/ppermute | solution.py:25
  257.6 17.0 %copy-start.3 = (bf16[256,1536]{1,0:T(8,128)(2,1)}, bf16[256,1536]{1,0:T(8,128)(2,1)S(1)}, u32[]{:S(2)}) copy-start(bf16[256,1536]{1,0:T(8,128)(2,1)S(1)} %collective-permute-done.9.left_high) | copy-start | bytes 2359300
  259.4 15.2 %copy-start.4 = (bf16[256,1536]{1,0:T(8,128)(2,1)}, bf16[256,1536]{1,0:T(8,128)(2,1)S(1)}, u32[]{:S(2)}) copy-start(bf16[256,1536]{1,0:T(8,128)(2,1)S(1)} %collective-permute-done.10.right_low) | copy-start | bytes 2359300
  273.1 1.5 copy-start.5
  274.6 0.9 copy-start.6
Sparse Core Ops, SparseCore 0:
  9.8 57.7 all-gather.2
  69.4 53.4 all-gather.4
  174.8 35.7 reduce-scatter.4
  220.1 52.1 reduce-scatter.2

commit v2 on v1

--- a/solution.py
+++ b/solution.py
@@ -84,19 +84,27 @@
     )(pick, *weight, tokens)
 
 
-def terms_kernel(pick, weight, rows, out):
-    held = (weight[...] * rows[...].astype(F32)).astype(BF16)
-    out[...] = dot(pick[...], held).astype(BF16)
+def column_loads(src, dst, sems, wide):
+    spans = [slice(n, n + wide) for n in range(0, src.shape[1], wide)]
+    return spans, start_loads([(src.at[:, c], dst.at[:, c]) for c in spans], sems)
+
+
+def terms_kernel(pick, weight, rows_hbm, out, rows_ref, sems):
+    spans, loads = column_loads(rows_hbm, rows_ref, sems, WIDE)
+    for cols, load in zip(spans, loads):
+        load.wait()
+        held = (weight[...] * rows_ref[:, cols].astype(F32)).astype(BF16)
+        out[:, cols] = dot(pick[...], held).astype(BF16)
 
 
 def token_terms(pick, weight, rows):
     out = jax.ShapeDtypeStruct((pick.shape[0], rows.shape[1]), BF16)
     return pl.pallas_call(
         terms_kernel,
-        grid=(rows.shape[1] // WIDE,),
         out_shape=out,
-        in_specs=[fixed(pick), fixed(weight), columns(rows, WIDE)],
-        out_specs=columns(out, WIDE),
+        in_specs=[whole(), whole(), pl.BlockSpec(memory_space=pltpu.HBM)],
+        out_specs=whole(),
+        scratch_shapes=[pltpu.VMEM(rows.shape, BF16), pltpu.SemaphoreType.DMA((rows.shape[1] // WIDE,))],
         compiler_params=params(),
         cost_estimate=cost(2 * pick.size * rows.shape[1], 2 * (pick.size + rows.size + out.size)),
     )(pick, weight, rows)
@@ -155,10 +163,11 @@
     )(rows, hidden, w_down)
 
 
-def down_kernel(hidden_t, outs, down):
-    part = down.shape[2]
-    for d in range(down.shape[0]):
-        down[d] = dot(hidden_t[...], outs[:, d * part : (d + 1) * part]).astype(BF16)
+def down_kernel(hidden_t, outs_hbm, down, outs, sems):
+    spans, loads = column_loads(outs_hbm, outs, sems, down.shape[2])
+    for d, (cols, load) in enumerate(zip(spans, loads)):
+        load.wait()
+        down[d] = dot(hidden_t[...], outs[:, cols]).astype(BF16)
 
 
 def down_terms(hidden_t, outs, ndp):
@@ -167,8 +176,9 @@
     return pl.pallas_call(
         down_kernel,
         out_shape=jax.ShapeDtypeStruct((ndp, ff, width // ndp), BF16),
-        in_specs=[whole()] * 2,
+        in_specs=[whole(), pl.BlockSpec(memory_space=pltpu.HBM)],
         out_specs=whole(),
+        scratch_shapes=[pltpu.VMEM(outs.shape, BF16), pltpu.SemaphoreType.DMA((ndp,))],
         compiler_params=params(),
         cost_estimate=cost(2 * count * ff * width, 2 * (count + ff) * width),
     )(hidden_t, outs)

time: 287 us -> 289 us (level)
  transfers between devices with their start and end apart: 20 -> 20, of which waited for: 11 -> 11; matrix products, arithmetic and copies ran while one was open for 7% -> 7% of each run, Pallas kernels for 19% -> 20%
where the time goes in v2:
time: 289 us; the launch traced here: 288 us
  waiting for transfers between devices  143 us (49%)
  Pallas kernels  70.7 us (24%)
  starting transfers between devices  35.7 us (12%)
  local copies, waits for them, and re-layouts  17.8 us (6%)
  between operations  14.1 us (5%)
  other arithmetic  7.02 us (2%)
    all_to_all x3, waiting for transfers between devices, swap(): lax.all_to_all(a.reshape(peers, -1, a.shape[1]), (Y, C), 0, 0, tiled=True)  69.7 us
    ppermute x13, waiting for transfers between devices, turn(): return lax.ppermute(a, axis, [(i, (i + step) % n) for i in range(n)])  54.8 us
    ppermute x13, starting transfers between devices, turn(): return lax.ppermute(a, axis, [(i, (i + step) % n) for i in range(n)])  23.7 us
    all_gather x1, waiting for transfers between devices, local(): all_tokens = lax.all_gather(tokens, Z, axis=0, tiled=True)  17.5 us
    pallas_call x2, Pallas kernels, pick_rows(): pl.pallas_call(pick_kernel, grid=(tokens.shape[1] // WIDE,), out_shape=ou...  13.4 us
    pallas_call x1, Pallas kernels, backward(): pl.pallas_call(functools.partial(backward_kernel, part), out_shape=[piece...  11.9 us
    all_to_all x3, starting transfers between devices, swap(): lax.all_to_all(a.reshape(peers, -1, a.shape[1]), (Y, C), 0, 0, tiled=True)  11.6 us
    pallas_call x1, Pallas kernels, hidden_units(): pl.pallas_call(hidden_kernel, out_shape=[jax.ShapeDtypeStruct((count, ff)...  10.8 us
  transfers between devices with their start and end apart: 20, of which 11 were waited for; matrix products, arithmetic and copies ran while one was open for 7% of the time, Pallas kernels for 20%

profile of v2, /device:TPU:6, one launch (start us, length us, event | category | flops | bytes accessed | tf_op | source)
XLA Modules:
  0.0 288.0 jit_solution(490380790257499828)
XLA Ops:
  9.3 3.3 %collective-permute-start.5 = (f32[8,128]{1,0:T(8,128)S(1)}, f32[8,128]{1,0:T(8,128)S(1)}, u32[]{:S(2)}, u32[]{:S(2)}) collective-permute-start(f32[8,128]{1,0:T(8,128)S(1)} %pad_maximum_fusion), channel_id=1, source_target_pairs={{0,4},{2,6},{4,8},{6,10},{8,12},{10,14},{12,0},{14,2},{1,5},{3,7},... | collective-permute-start | bytes 12296 | tf_op jit(solution)/shard_map/ppermute | solution.py:25
  12.6 4.9 %collective-permute-start.4 = (f32[8,128]{1,0:T(8,128)S(1)}, f32[8,128]{1,0:T(8,128)S(1)}, u32[]{:S(2)}, u32[]{:S(2)}) collective-permute-start(f32[8,128]{1,0:T(8,128)S(1)} %pad_maximum_fusion), channel_id=1, source_target_pairs={{0,6},{2,8},{4,10},{6,12},{8,14},{10,0},{12,2},{14,4},{1,7},{3,9},... | collective-permute-start | bytes 12296 | tf_op jit(solution)/shard_map/ppermute | solution.py:25
  18.5 4.5 %collective-permute-start.2 = (f32[8,128]{1,0:T(8,128)S(1)}, f32[8,128]{1,0:T(8,128)S(1)}, u32[]{:S(2)}, u32[]{:S(2)}) collective-permute-start(f32[8,128]{1,0:T(8,128)S(1)} %pad_maximum_fusion), channel_id=1, source_target_pairs={{0,10},{2,12},{4,14},{6,0},{8,2},{10,4},{12,6},{14,8},{1,11},{3,13... | collective-permute-start | bytes 12296 | tf_op jit(solution)/shard_map/ppermute | solution.py:25
  25.7 4.7 %copy.28 = bf16[1,768,2048]{1,2,0:T(8,128)(2,1)} copy(bf16[1,768,2048]{2,1,0:T(8,128)(2,1)} %param.14) | data formatting | bytes 6291456 | tf_op args[6]
  30.4 1.7 collective-permute-start.1
  32.1 2.9 %collective-permute-done.1 = f32[8,128]{1,0:T(8,128)S(1)} collective-permute-done((f32[8,128]{1,0:T(8,128)S(1)}, f32[8,128]{1,0:T(8,128)S(1)}, u32[]{:S(2)}, u32[]{:S(2)}) %collective-permute-start.1) | collective-permute-done | bytes 4128 | tf_op jit(solution)/shard_map/ppermute | solution.py:25
  36.1 4.0 %collective-permute-done.6 = f32[8,128]{1,0:T(8,128)S(1)} collective-permute-done((f32[8,128]{1,0:T(8,128)S(1)}, f32[8,128]{1,0:T(8,128)S(1)}, u32[]{:S(2)}, u32[]{:S(2)}) %collective-permute-start.6) | collective-permute-done | bytes 4128 | tf_op jit(solution)/shard_map/ppermute | solution.py:25
  41.0 1.9 eq.75
  42.9 2.2 copy.25
  47.7 2.5 copy.27.pick
  50.2 17.5 %all-gather.3.cloned.1.call-done.refs_0_ = bf16[1024,2048]{1,0:T(8,128)(2,1)} async-done(((bf16[128,2048]{1,0:T(8,128)(2,1)}), bf16[1024,2048]{1,0:T(8,128)(2,1)}) %all-gather.3.cloned.1.call-update) | async-done | bytes 4194320 | tf_op jit(solution)/shard_map/all_gather | solution.py:306
  67.6 6.7 %shard_map.111 = bf16[640,2048]{1,0:T(8,128)(2,1)} custom-call(bf16[640,1024]{1,0:T(8,128)(2,1)} %copy.27.pick, bf16[1024,2048]{1,0:T(8,128)(2,1)} %all-gather.3.cloned.1.call-done.refs_0_), custom_call_target="tpu_custom_call" | custom-call | flops 2684354560 | bytes 8126464 | tf_op jit(solution)/shard_map/pallas_call | solution.py:76
  74.3 4.3 %all-to-all-start = ((bf16[8,80,2048]{2,1,0:T(8,128)(2,1)}), bf16[8,80,2048]{2,1,0:T(8,128)(2,1)S(1)}, u32[]{:S(2)}, u32[]{:S(2)}) async-start(bf16[8,80,2048]{2,1,0:T(8,128)(2,1)} %bitcast.64), calls=%async_computation | async-start | bytes 5242880 | tf_op jit(solution)/shard_map/all_to_all | solution.py:30
  79.5 31.9 %all-to-all-done = bf16[8,80,2048]{2,1,0:T(8,128)(2,1)S(1)} async-done(((bf16[8,80,2048]{2,1,0:T(8,128)(2,1)}), bf16[8,80,2048]{2,1,0:T(8,128)(2,1)S(1)}, u32[]{:S(2)}, u32[]{:S(2)}) %all-to-all-start) | async-done | bytes 2621472 | tf_op jit(solution)/shard_map/all_to_all | solution.py:30
  112.9 10.8 %shard_map.112 = (bf16[640,768]{1,0:T(8,128)(2,1)}, f32[640,768]{1,0:T(8,128)}, f32[640,768]{1,0:T(8,128)}) custom-call(bf16[640,2048]{1,0:T(8,128)(2,1)} %bitcast.61, bf16[2048,768]{1,0:T(8,128)(2,1)} %bitcast.69, bf16[2048,768]{1,0:T(8,128)(2,1)} %bitcast.70), custom_call_target="tpu_custom_call" | custom-call | flops 4026531840 | bytes 13828096 | tf_op jit(solution)/shard_map/pallas_call | solution.py:134
  123.7 6.7 %shard_map.113 = bf16[640,2048]{1,0:T(8,128)(2,1)} custom-call(bf16[640,1024]{1,0:T(8,128)(2,1)} %copy.27.pick, f32[640,1]{1,0:T(8,128)} %copy.32.refs_0_.weight, bf16[1024,2048]{1,0:T(8,128)(2,1)} %all-gather.5.cloned.1.call-done.refs_1_), custom_call_target="tpu_custom_call" | custom-call | flops 2684354560 | bytes 8126464 | tf_op jit(solution)/shard_map/pallas_call | solution.py:76
  130.4 3.6 %all-to-all-start.2 = ((bf16[8,80,2048]{2,1,0:T(8,128)(2,1)}), bf16[8,80,2048]{2,1,0:T(8,128)(2,1)S(1)}, u32[]{:S(2)}, u32[]{:S(2)}) async-start(bf16[8,80,2048]{2,1,0:T(8,128)(2,1)} %bitcast.63), calls=%async_computation.2 | async-start | bytes 5242880 | tf_op jit(solution)/shard_map/all_to_all | solution.py:30
  134.1 7.5 %shard_map.114 = (bf16[640,2048]{1,0:T(8,128)(2,1)}, bf16[2048,640]{1,0:T(8,128)(2,1)}, bf16[768,640]{1,0:T(8,128)(2,1)}) custom-call(bf16[640,2048]{1,0:T(8,128)(2,1)} %bitcast.62, bf16[640,768]{1,0:T(8,128)(2,1)} %get-tuple-element.28.hidden_ref, bf16[768,2048]{1,0:T(8,128)(2,1)} %bitcast.59), custom_call_target="tpu_custom_call" | custom-call | flops 2013265920 | bytes 11010048 | tf_op jit(solution)/shard_map/pallas_call | solution.py:156
  141.7 25.1 %all-to-all-done.2 = bf16[8,80,2048]{2,1,0:T(8,128)(2,1)S(1)} async-done(((bf16[8,80,2048]{2,1,0:T(8,128)(2,1)}), bf16[8,80,2048]{2,1,0:T(8,128)(2,1)S(1)}, u32[]{:S(2)}, u32[]{:S(2)}) %all-to-all-start.2) | async-done | bytes 2621472 | tf_op jit(solution)/shard_map/all_to_all | solution.py:30
  168.3 7.1 %shard_map.115 = bf16[4,768,512]{2,1,0:T(8,128)(2,1)} custom-call(bf16[768,640]{1,0:T(8,128)(2,1)} %get-tuple-element.31.hidden_t, bf16[640,2048]{1,0:T(8,128)(2,1)} %bitcast.57), custom_call_target="tpu_custom_call" | custom-call | flops 2013265920 | bytes 5767168 | tf_op jit(solution)/shard_map/pallas_call | solution.py:176
  175.4 3.6 %all-to-all-start.1 = ((bf16[8,80,2048]{2,1,0:T(8,128)(2,1)}), bf16[8,80,2048]{2,1,0:T(8,128)(2,1)S(1)}, u32[]{:S(2)}, u32[]{:S(2)}) async-start(bf16[8,80,2048]{2,1,0:T(8,128)(2,1)} %bitcast.20), calls=%async_computation.1 | async-start | bytes 5242880 | tf_op jit(solution)/shard_map/all_to_all | solution.py:30
  179.9 11.9 %shard_map.116 = (bf16[256,1536]{1,0:T(8,128)(2,1)}, bf16[256,1536]{1,0:T(8,128)(2,1)}, bf16[640,1536]{1,0:T(8,128)(2,1)}) custom-call(s32[4]{0:T(128)} %and_select_fusion.to, bf16[640,2048]{1,0:T(8,128)(2,1)} %bitcast.58, bf16[2048,768]{1,0:T(8,128)(2,1)} %bitcast.55, f32[640,768]{1,0:T(8,128)} %get-tuple-element.33.refs_2_, ...), custom_call_target="tpu_custom_call" | custom-call | flops 3019898880 | bytes 16252928 | tf_op jit(solution)/shard_map/pallas_call | solution.py:227
  191.7 7.4 %shard_map.117 = (bf16[256,1536]{1,0:T(8,128)(2,1)}, bf16[256,1536]{1,0:T(8,128)(2,1)}, bf16[256,1536]{1,0:T(8,128)(2,1)}, bf16[256,1536]{1,0:T(8,128)(2,1)}, bf16[512,1536]{1,0:T(8,128)(2,1)}) custom-call(s32[4]{0:T(128)} %and_select_fusion.to, bf16[2048,640]{1,0:T(8,128)(2,1)} %get-tuple-element.30.refs_4_.rows_t, bf16[640,1536]{1,0:T(8,128)(2,1)} %get-tuple-element.35.back_ref), custom_call_target="tpu_custom_call" | custom-call | flops 3019898880 | bytes 9306112 | tf_op jit(solution)/shard_map/pallas_call | solution.py:251
  199.1 12.7 %all-to-all-done.1 = bf16[8,80,2048]{2,1,0:T(8,128)(2,1)S(1)} async-done(((bf16[8,80,2048]{2,1,0:T(8,128)(2,1)}), bf16[8,80,2048]{2,1,0:T(8,128)(2,1)S(1)}, u32[]{:S(2)}, u32[]{:S(2)}) %all-to-all-start.1) | async-done | bytes 2621472 | tf_op jit(solution)/shard_map/all_to_all | solution.py:30
  213.3 8.8 %shard_map.118 = bf16[1024,2048]{1,0:T(8,128)(2,1)} custom-call(bf16[1024,640]{1,0:T(8,128)(2,1)} %fusion.14.pick, f32[640,1]{1,0:T(8,128)} %copy.32.refs_0_.weight, bf16[640,2048]{1,0:T(8,128)(2,1)} %bitcast.60), custom_call_target="tpu_custom_call" | custom-call | flops 2684354560 | bytes 8126464 | tf_op jit(solution)/shard_map/pallas_call | solution.py:102
  224.2 1.8 collective-permute-start.9
  226.3 16.6 %collective-permute-done.7 = bf16[256,1536]{1,0:T(8,128)(2,1)S(1)} collective-permute-done((bf16[256,1536]{1,0:T(8,128)(2,1)}, bf16[256,1536]{1,0:T(8,128)(2,1)S(1)}, u32[]{:S(2)}, u32[]{:S(2)}) %collective-permute-start.7) | collective-permute-done | bytes 786464 | tf_op jit(solution)/shard_map/ppermute | solution.py:25
  243.1 1.8 collective-permute-start.8
  245.5 14.3 %collective-permute-done.9.left_high = bf16[256,1536]{1,0:T(8,128)(2,1)S(1)} collective-permute-done((bf16[256,1536]{1,0:T(8,128)(2,1)S(1)}, bf16[256,1536]{1,0:T(8,128)(2,1)S(1)}, u32[]{:S(2)}, u32[]{:S(2)}) %collective-permute-start.9) | collective-permute-done | bytes 786464 | tf_op jit(solution)/shard_map/ppermute | solution.py:25
  259.7 1.8 collective-permute-done.10.right_low
  261.5 13.7 %collective-permute-done.8.left_low = bf16[256,1536]{1,0:T(8,128)(2,1)S(1)} collective-permute-done((bf16[256,1536]{1,0:T(8,128)(2,1)S(1)}, bf16[256,1536]{1,0:T(8,128)(2,1)S(1)}, u32[]{:S(2)}, u32[]{:S(2)}) %collective-permute-start.8) | collective-permute-done | bytes 786464 | tf_op jit(solution)/shard_map/ppermute | solution.py:25
  277.6 3.9 %shard_map.119 = (bf16[512,768]{1,0:T(8,128)(2,1)}, bf16[512,768]{1,0:T(8,128)(2,1)}) custom-call(bf16[512,1536]{1,0:T(8,128)(2,1)} %get-tuple-element.41.me, bf16[256,1536]{1,0:T(8,128)(2,1)} %copy-done.5, bf16[256,1536]{1,0:T(8,128)(2,1)} %copy-done.3, bf16[256,1536]{1,0:T(8,128)(2,1)} %copy-done.4, bf16[256,1536]{1,0:T(8,128)(2,1)} %copy-done.6), custom_call_target="tpu_custom_call" | custom-call | flops 2359296 | bytes 6291456 | tf_op jit(solution)/shard_map/pallas_call | solution.py:283
  (89 shorter events, 22.1 us)
Async XLA Ops:
  7.2 60.5 %all-gather.3.cloned.1.call-start = ((), (), s32[]{:S(2)}) async-start(), calls=%async_computation.5 | async-start | bytes 4718592 | tf_op jit(solution)/shard_map/all_gather | solution.py:306
  7.9 115.8 %all-gather.5.cloned.1.call-start = ((), (), s32[]{:S(2)}) async-start(), calls=%async_computation.6 | async-start | bytes 4718592 | tf_op jit(solution)/shard_map/all_gather | solution.py:333
  9.3 26.7 %collective-permute-start.5 = (f32[8,128]{1,0:T(8,128)S(1)}, f32[8,128]{1,0:T(8,128)S(1)}, u32[]{:S(2)}, u32[]{:S(2)}) collective-permute-start(f32[8,128]{1,0:T(8,128)S(1)} %pad_maximum_fusion), channel_id=1, source_target_pairs={{0,4},{2,6},{4,8},{6,10},{8,12},{10,14},{12,0},{14,2},{1,5},{3,7},... | collective-permute-start | bytes 12296 | tf_op jit(solution)/shard_map/ppermute | solution.py:25
  12.6 23.5 %collective-permute-start.4 = (f32[8,128]{1,0:T(8,128)S(1)}, f32[8,128]{1,0:T(8,128)S(1)}, u32[]{:S(2)}, u32[]{:S(2)}) collective-permute-start(f32[8,128]{1,0:T(8,128)S(1)} %pad_maximum_fusion), channel_id=1, source_target_pairs={{0,6},{2,8},{4,10},{6,12},{8,14},{10,0},{12,2},{14,4},{1,7},{3,9},... | collective-permute-start | bytes 12296 | tf_op jit(solution)/shard_map/ppermute | solution.py:25
  17.5 18.5 %collective-permute-start.3 = (f32[8,128]{1,0:T(8,128)S(1)}, f32[8,128]{1,0:T(8,128)S(1)}, u32[]{:S(2)}, u32[]{:S(2)}) collective-permute-start(f32[8,128]{1,0:T(8,128)S(1)} %pad_maximum_fusion), channel_id=1, source_target_pairs={{0,8},{2,10},{4,12},{6,14},{8,0},{10,2},{12,4},{14,6},{1,9},{3,11}... | collective-permute-start | bytes 12296 | tf_op jit(solution)/shard_map/ppermute | solution.py:25
  18.5 17.5 %collective-permute-start.2 = (f32[8,128]{1,0:T(8,128)S(1)}, f32[8,128]{1,0:T(8,128)S(1)}, u32[]{:S(2)}, u32[]{:S(2)}) collective-permute-start(f32[8,128]{1,0:T(8,128)S(1)} %pad_maximum_fusion), channel_id=1, source_target_pairs={{0,10},{2,12},{4,14},{6,0},{8,2},{10,4},{12,6},{14,8},{1,11},{3,13... | collective-permute-start | bytes 12296 | tf_op jit(solution)/shard_map/ppermute | solution.py:25
  23.0 7.4 %collective-permute-start = (f32[8,128]{1,0:T(8,128)S(1)}, f32[8,128]{1,0:T(8,128)S(1)}, u32[]{:S(2)}, u32[]{:S(2)}) collective-permute-start(f32[8,128]{1,0:T(8,128)S(1)} %pad_maximum_fusion), channel_id=1, source_target_pairs={{0,14},{2,0},{4,2},{6,4},{8,6},{10,8},{12,10},{14,12},{1,15},{3,1}... | collective-permute-start | bytes 12296 | tf_op jit(solution)/shard_map/ppermute | solution.py:25
  25.7 14.4 %copy-start.9 = (f32[128,4]{0,1:T(4,128)S(1)}, f32[128,4]{0,1:T(4,128)}, u32[]{:S(2)}) copy-start(f32[128,4]{0,1:T(4,128)} %param.10) | copy-start | bytes 6148
  30.4 4.6 %collective-permute-start.1 = (f32[8,128]{1,0:T(8,128)S(1)}, f32[8,128]{1,0:T(8,128)S(1)}, u32[]{:S(2)}, u32[]{:S(2)}) collective-permute-start(f32[8,128]{1,0:T(8,128)S(1)} %pad_maximum_fusion), channel_id=1, source_target_pairs={{0,12},{2,14},{4,0},{6,2},{8,4},{10,6},{12,8},{14,10},{1,13},{3,15... | collective-permute-start | bytes 12296 | tf_op jit(solution)/shard_map/ppermute | solution.py:25
  35.0 5.1 %collective-permute-start.6 = (f32[8,128]{1,0:T(8,128)S(1)}, f32[8,128]{1,0:T(8,128)S(1)}, u32[]{:S(2)}, u32[]{:S(2)}) collective-permute-start(f32[8,128]{1,0:T(8,128)S(1)} %pad_maximum_fusion), channel_id=1, source_target_pairs={{0,2},{2,4},{4,6},{6,8},{8,10},{10,12},{12,14},{14,0},{1,3},{3,5},... | collective-permute-start | bytes 12296 | tf_op jit(solution)/shard_map/ppermute | solution.py:25
  74.3 37.1 %all-to-all-start = ((bf16[8,80,2048]{2,1,0:T(8,128)(2,1)}), bf16[8,80,2048]{2,1,0:T(8,128)(2,1)S(1)}, u32[]{:S(2)}, u32[]{:S(2)}) async-start(bf16[8,80,2048]{2,1,0:T(8,128)(2,1)} %bitcast.64), calls=%async_computation | async-start | bytes 5242880 | tf_op jit(solution)/shard_map/all_to_all | solution.py:30
  111.4 1.5 copy-start.2
  130.4 36.4 %all-to-all-start.2 = ((bf16[8,80,2048]{2,1,0:T(8,128)(2,1)}), bf16[8,80,2048]{2,1,0:T(8,128)(2,1)S(1)}, u32[]{:S(2)}, u32[]{:S(2)}) async-start(bf16[8,80,2048]{2,1,0:T(8,128)(2,1)} %bitcast.63), calls=%async_computation.2 | async-start | bytes 5242880 | tf_op jit(solution)/shard_map/all_to_all | solution.py:30
  134.1 147.4 %reduce-scatter.5.cloned.1.call-start = ((), (), s32[]{:S(2)}) async-start(), calls=%async_computation.8 | async-start | bytes 3932160 | tf_op jit(solution)/shard_map/reduce_scatter | solution.py:345
  166.8 1.5 copy-start
  175.4 36.4 %all-to-all-start.1 = ((bf16[8,80,2048]{2,1,0:T(8,128)(2,1)}), bf16[8,80,2048]{2,1,0:T(8,128)(2,1)S(1)}, u32[]{:S(2)}, u32[]{:S(2)}) async-start(bf16[8,80,2048]{2,1,0:T(8,128)(2,1)} %bitcast.20), calls=%async_computation.1 | async-start | bytes 5242880 | tf_op jit(solution)/shard_map/all_to_all | solution.py:30
  179.1 102.4 %reduce-scatter.3.cloned.1.call-start = ((), (), s32[]{:S(2)}) async-start(), calls=%async_computation.7 | async-start | bytes 4718592 | tf_op jit(solution)/shard_map/reduce_scatter | solution.py:351
  211.8 1.5 copy-start.1
  222.1 2.2 copy-start.11
  222.1 3.9 %copy-start.10 = (bf16[256,1536]{1,0:T(8,128)(2,1)S(1)}, bf16[256,1536]{1,0:T(8,128)(2,1)}, u32[]{:S(2)}) copy-start(bf16[256,1536]{1,0:T(8,128)(2,1)} %get-tuple-element.38) | copy-start | bytes 2359300
  222.1 20.8 %copy-start.8 = (bf16[256,1536]{1,0:T(8,128)(2,1)S(1)}, bf16[256,1536]{1,0:T(8,128)(2,1)}, u32[]{:S(2)}) copy-start(bf16[256,1536]{1,0:T(8,128)(2,1)} %get-tuple-element.36) | copy-start | bytes 2359300
  222.1 22.8 %copy-start.7 = (bf16[256,1536]{1,0:T(8,128)(2,1)S(1)}, bf16[256,1536]{1,0:T(8,128)(2,1)}, u32[]{:S(2)}) copy-start(bf16[256,1536]{1,0:T(8,128)(2,1)} %get-tuple-element.39) | copy-start | bytes 2359300
  222.1 20.7 %collective-permute-start.7 = (bf16[256,1536]{1,0:T(8,128)(2,1)}, bf16[256,1536]{1,0:T(8,128)(2,1)S(1)}, u32[]{:S(2)}, u32[]{:S(2)}) collective-permute-start(bf16[256,1536]{1,0:T(8,128)(2,1)} %get-tuple-element.42), channel_id=1, source_target_pairs={{0,64},{64,128},{128,192},{192,0},{1,65},{65,129},{129,193},{193,1... | collective-permute-start | bytes 2359304 | tf_op jit(solution)/shard_map/ppermute | solution.py:25
  222.8 22.2 %collective-permute-start.11 = (bf16[256,1536]{1,0:T(8,128)(2,1)}, bf16[256,1536]{1,0:T(8,128)(2,1)S(1)}, u32[]{:S(2)}, u32[]{:S(2)}) collective-permute-start(bf16[256,1536]{1,0:T(8,128)(2,1)} %get-tuple-element.43), channel_id=1, source_target_pairs={{0,192},{64,0},{128,64},{192,128},{1,193},{65,1},{129,65},{193,129... | collective-permute-start | bytes 2359304 | tf_op jit(solution)/shard_map/ppermute | solution.py:25
  224.2 35.5 %collective-permute-start.9 = (bf16[256,1536]{1,0:T(8,128)(2,1)S(1)}, bf16[256,1536]{1,0:T(8,128)(2,1)S(1)}, u32[]{:S(2)}, u32[]{:S(2)}) collective-permute-start(bf16[256,1536]{1,0:T(8,128)(2,1)S(1)} %copy-done.11), channel_id=1, source_target_pairs={{0,64},{64,128},{128,192},{192,0},{1,65},{65,129},{129,193},{193,1... | collective-permute-start | bytes 2359304 | tf_op jit(solution)/shard_map/ppermute | solution.py:25
  226.0 35.5 %collective-permute-start.10 = (bf16[256,1536]{1,0:T(8,128)(2,1)S(1)}, bf16[256,1536]{1,0:T(8,128)(2,1)S(1)}, u32[]{:S(2)}, u32[]{:S(2)}) collective-permute-start(bf16[256,1536]{1,0:T(8,128)(2,1)S(1)} %copy-done.10), channel_id=1, source_target_pairs={{0,192},{64,0},{128,64},{192,128},{1,193},{65,1},{129,65},{193,129... | collective-permute-start | bytes 2359304 | tf_op jit(solution)/shard_map/ppermute | solution.py:25
  243.1 32.1 %collective-permute-start.8 = (bf16[256,1536]{1,0:T(8,128)(2,1)S(1)}, bf16[256,1536]{1,0:T(8,128)(2,1)S(1)}, u32[]{:S(2)}, u32[]{:S(2)}) collective-permute-start(bf16[256,1536]{1,0:T(8,128)(2,1)S(1)} %add_convert_fusion.1), channel_id=1, source_target_pairs={{0,64},{64,128},{128,192},{192,0},{1,65},{65,129},{129,193},{193,1... | collective-permute-start | bytes 2359304 | tf_op jit(solution)/shard_map/ppermute | solution.py:25
  245.1 31.6 %collective-permute-start.12 = (bf16[256,1536]{1,0:T(8,128)(2,1)S(1)}, bf16[256,1536]{1,0:T(8,128)(2,1)S(1)}, u32[]{:S(2)}, u32[]{:S(2)}) collective-permute-start(bf16[256,1536]{1,0:T(8,128)(2,1)S(1)} %add_convert_fusion), channel_id=1, source_target_pairs={{0,192},{64,0},{128,64},{192,128},{1,193},{65,1},{129,65},{193,129... | collective-permute-start | bytes 2359304 | tf_op jit(solution)/shard_map/ppermute | solution.py:25
  259.7 17.0 %copy-start.3 = (bf16[256,1536]{1,0:T(8,128)(2,1)}, bf16[256,1536]{1,0:T(8,128)(2,1)S(1)}, u32[]{:S(2)}) copy-start(bf16[256,1536]{1,0:T(8,128)(2,1)S(1)} %collective-permute-done.9.left_high) | copy-start | bytes 2359300
  261.5 15.2 %copy-start.4 = (bf16[256,1536]{1,0:T(8,128)(2,1)}, bf16[256,1536]{1,0:T(8,128)(2,1)S(1)}, u32[]{:S(2)}) copy-start(bf16[256,1536]{1,0:T(8,128)(2,1)S(1)} %collective-permute-done.10.right_low) | copy-start | bytes 2359300
  275.2 1.5 copy-start.5
  276.7 0.9 copy-start.6
Sparse Core Ops, SparseCore 0:
  9.8 57.7 all-gather.2
  69.4 53.4 all-gather.4
  175.5 35.7 reduce-scatter.4
  222.3 52.1 reduce-scatter.2
